TPU v7x, 256 devices: a whole 4x4x8 slice. The times are simulated.
256 devices in a mesh: seq: 64 (over x_lo, z, y), rep: 4 (over x_hi, core).
Axes of the slice: x: 4 (x_hi: 2, x_lo: 2; x = x_hi * 2 + x_lo), y: 4, z: 8, core: 2. Of those that a mesh axis runs over, the one named last changes fastest.
Arguments:
- queries: bfloat16 [32768, 4096], P('seq', 'rep'), may hold values from -12 to 12
- keys: bfloat16 [32768, 1024], P('seq', 'rep'), may hold values from -6 to 6
- values: bfloat16 [32768, 1024], P('seq', 'rep'), may hold values from -6 to 6
- output_gradient: bfloat16 [32768, 4096], P('seq'), may hold values from -6 to 6
- output_weight: bfloat16 [4096, 4096], P('rep'), may hold values from -0.09375 to 0.09375
- adapter_down: bfloat16 [4096, 32], P('rep'), may hold values from -0.09375 to 0.09375
- adapter_up: bfloat16 [32, 4096], replicated, may hold values from -0.09375 to 0.09375
- positions: int32 [32768], P('seq'), may hold values from 0 to 32767, as said below
- block_pair_mask: int32 [64, 2, 2, 2], P('seq'), may hold values from 0 to 2, as said below
Outputs:
- query_gradient: bfloat16 [32768, 4096], P('seq', 'rep')
- key_gradient: bfloat16 [32768, 1024], P('seq', 'rep')
- value_gradient: bfloat16 [32768, 1024], P('seq', 'rep')
- adapter_down_gradient: float32 [4096, 32], P('rep')
- adapter_up_gradient: float32 [32, 4096], replicated
Inputs may be any that keep to these rules, and one draw needn't show every extreme that they name: The sequence is cut into blocks of 256 consecutive positions, and each device holds two such blocks, in a drawn order; every position occurs once. block_pair_mask[d, 0, a, a] = 2; every other entry is 1 where all positions of the key half precede those of the query half, and 0 where all follow.
All inputs are finite; a program needn't handle non-finite values.
Results may differ from a plain program's by a relative error of at most 0.017.
Values may be sent and summed in bfloat16 or wider, within the bound.
A program may use at most 128 MiB of HBM per device.

v0:
```python
import jax
import jax.numpy as jnp
from jax import lax
from jax.sharding import PartitionSpec as P

HEAD_SIZE = 128


def shifted(x, axis, by):
    size = lax.axis_size(axis)
    return lax.ppermute(x, axis, [(i, (i + by) % size) for i in range(size)])


def angles(pos, width):
    freq = 1000000.0 ** (-(jnp.arange(width // 2).astype(jnp.float32) * 2.0 / width))
    phase = pos.astype(jnp.float32)[:, None] * freq[None, :]
    return (jnp.cos(phase), jnp.sin(phase))


def rotate(x, cosine, sine):
    half_w = x.shape[-1] // 2
    first, second = (x[..., :half_w], x[..., half_w:])
    c_term, s_term = (cosine[:, None, :], sine[:, None, :])
    return jnp.concatenate([first * c_term - second * s_term, second * c_term + first * s_term], -1)


def unrotate(x, cosine, sine):
    half_w = x.shape[-1] // 2
    first, second = (x[..., :half_w], x[..., half_w:])
    c_term, s_term = (cosine[:, None, :], sine[:, None, :])
    return jnp.concatenate([first * c_term + second * s_term, second * c_term - first * s_term], -1)


def tile_modes(modes, half_rows):
    return jnp.broadcast_to(modes[:, None, :, None], (2, half_rows, 2, half_rows)).reshape(
        2 * half_rows, 2 * half_rows
    )


def scores(q_rot, k_rot, allowed):
    raw = jnp.einsum("tkgw,ukw->kgtu", q_rot, k_rot, preferred_element_type=jnp.float32)
    raw = raw * q_rot.shape[-1] ** (-0.5)
    return jnp.where(allowed[None, None], raw, -jnp.inf)


def step_back(s_block, lse, q_rot, k_rot, v_blk, attention_gradient, delta):
    scale = q_rot.shape[-1] ** (-0.5)
    p_wide = jnp.exp(s_block - lse[..., None])
    p_narrow = p_wide.astype(jnp.bfloat16)
    d_prob = jnp.einsum(
        "tkgw,ukw->kgtu", attention_gradient, v_blk, preferred_element_type=jnp.float32
    )
    d_score = (p_wide * (d_prob - delta[..., None])).astype(jnp.bfloat16)
    dq_part = (
        jnp.einsum("kgtu,ukw->tkgw", d_score, k_rot, preferred_element_type=jnp.float32) * scale
    )
    dk_part = (
        jnp.einsum("kgtu,tkgw->ukw", d_score, q_rot, preferred_element_type=jnp.float32) * scale
    )
    dv_part = jnp.einsum(
        "kgtu,tkgw->ukw", p_narrow, attention_gradient, preferred_element_type=jnp.float32
    )
    return (dq_part, dk_part, dv_part)


def shards(
    queries,
    keys,
    values,
    output_gradient,
    output_weight,
    adapter_down,
    adapter_up,
    positions,
    block_pair_mask,
):
    rows = queries.shape[0]
    half_rows = rows // 2
    width = HEAD_SIZE
    kv_local = keys.shape[1] // width
    q_local = queries.shape[1] // width
    groups = q_local // kv_local
    cosine, sine = angles(positions, width)
    q_rot = rotate(queries.reshape(rows, q_local, width).astype(jnp.float32), cosine, sine)
    q_rot = q_rot.astype(jnp.bfloat16).reshape(rows, kv_local, groups, width)
    k_rot = rotate(keys.reshape(rows, kv_local, width).astype(jnp.float32), cosine, sine).astype(
        jnp.bfloat16
    )
    v_own = values.reshape(rows, kv_local, width)
    k_prev, v_prev = shifted((k_rot, v_own), "seq", 1)
    modes = block_pair_mask[0]
    own_code = tile_modes(modes[0], half_rows)
    own_allowed = (own_code == 1) | (own_code == 2) & (positions[None, :] <= positions[:, None])
    prev_allowed = tile_modes(modes[1], half_rows) == 1
    s_own = scores(q_rot, k_rot, own_allowed)
    s_prev = scores(q_rot, k_prev, prev_allowed)
    lse = jnp.logaddexp(jax.nn.logsumexp(s_own, -1), jax.nn.logsumexp(s_prev, -1))
    p_own = jnp.exp(s_own - lse[..., None]).astype(jnp.bfloat16)
    p_prev = jnp.exp(s_prev - lse[..., None]).astype(jnp.bfloat16)
    attn4 = jnp.einsum("kgtu,ukw->tkgw", p_own, v_own, preferred_element_type=jnp.float32)
    attn4 = (
        attn4 + jnp.einsum("kgtu,ukw->tkgw", p_prev, v_prev, preferred_element_type=jnp.float32)
    ).astype(jnp.bfloat16)
    attention_output = attn4.reshape(rows, q_local * width)
    adapter_middle = lax.psum(
        jnp.dot(attention_output, adapter_down, preferred_element_type=jnp.float32), "rep"
    ).astype(jnp.bfloat16)
    backward_result = lax.dot_general(
        output_gradient, adapter_up, (((1,), (1,)), ((), ())), preferred_element_type=jnp.float32
    ).astype(jnp.bfloat16)
    a_term = lax.dot_general(
        attention_output,
        backward_result,
        (((0,), (0,)), ((), ())),
        preferred_element_type=jnp.float32,
    )
    b_term = lax.dot_general(
        adapter_middle,
        output_gradient,
        (((0,), (0,)), ((), ())),
        preferred_element_type=jnp.float32,
    )
    down_factor_sum, up_factor_sum = lax.psum((a_term, b_term), "seq")
    adapter_up_gradient = 2.0 * up_factor_sum
    adapter_down_gradient = 2.0 * down_factor_sum
    attention_gradient = lax.dot_general(
        output_gradient, output_weight, (((1,), (1,)), ((), ())), preferred_element_type=jnp.float32
    )
    attention_gradient = attention_gradient + 2.0 * lax.dot_general(
        backward_result, adapter_down, (((1,), (1,)), ((), ())), preferred_element_type=jnp.float32
    )
    d_attn4 = attention_gradient.astype(jnp.bfloat16).reshape(rows, kv_local, groups, width)
    delta = jnp.sum(d_attn4.astype(jnp.float32) * attn4.astype(jnp.float32), -1).transpose(1, 2, 0)
    dq_own, dk_own, dv_own = step_back(s_own, lse, q_rot, k_rot, v_own, d_attn4, delta)
    dq_prev, dk_prev, dv_prev = step_back(s_prev, lse, q_rot, k_prev, v_prev, d_attn4, delta)
    dk_back, dv_back = shifted(
        (dk_prev.astype(jnp.bfloat16), dv_prev.astype(jnp.bfloat16)), "seq", -1
    )
    dq_rot = (dq_own + dq_prev).reshape(rows, q_local, width)
    query_gradient = (
        unrotate(dq_rot, cosine, sine).astype(jnp.bfloat16).reshape(rows, q_local * width)
    )
    key_gradient = (
        unrotate(dk_own + dk_back.astype(jnp.float32), cosine, sine)
        .astype(jnp.bfloat16)
        .reshape(rows, kv_local * width)
    )
    value_gradient = (
        (dv_own + dv_back.astype(jnp.float32)).astype(jnp.bfloat16).reshape(rows, kv_local * width)
    )
    return (
        query_gradient,
        key_gradient,
        value_gradient,
        adapter_down_gradient,
        adapter_up_gradient,
    )


def solution(mesh):
    placed = (
        P("seq", "rep"),
        P("seq", "rep"),
        P("seq", "rep"),
        P("seq", None),
        P("rep", None),
        P("rep", None),
        P(),
        P("seq"),
        P("seq", None, None, None),
    )
    return jax.shard_map(
        shards,
        mesh=mesh,
        in_specs=placed,
        out_specs=(P("seq", "rep"), P("seq", "rep"), P("seq", "rep"), P("rep", None), P()),
        check_vma=False,
    )
```

profile of v0, /device:TPU:24, one launch (start us, length us, event | category | flops | bytes accessed | tf_op | source)
XLA Modules:
  0.0 691.3 jit_solution(7191951776646618831)
XLA Ops:
  16.4 2.0 fusion.34
  20.8 2.4 subtract_convert_fusion.1
  23.8 5.6 fusion.6
  30.4 3.7 convolution_convert_fusion
  34.1 8.9 %fusion.36 = f32[512,1024]{1,0:T(8,128)S(1)} fusion(bf16[512,4096]{1,0:T(8,128)(2,1)} %param.12, bf16[1024,4096]{1,0:T(8,128)(2,1)} %param.13), kind=kOutput, calls=%fused_computation.77 | convolution fusion | flops 4294967296 | bytes 14680064 | tf_op jit(solution)/shard_map/dot_general | solution.py:126
  43.1 1.8 exponential_reduce_fusion.1
  46.6 2.4 fusion.7
  49.0 1.8 exponential_reduce_fusion
  50.9 6.8 fusion.29
  57.7 3.6 multiply_reduce_fusion
  62.8 18.5 %psum.22 = bf16[512,32]{1,0:T(8,128)(2,1)S(1)} all-reduce(f32[512,32]{1,0:T(8,128)S(1)} %fusion.38), channel_id=1, replica_groups=mesh['seq'=64,'rep'=4] {'rep'}, use_global_device_ids=true, to_apply=%region_6.7 | all-reduce | flops 16384 | bytes 98304 | tf_op jit(solution)/shard_map/psum | solution.py:105
  81.4 3.8 fusion.39
  85.2 6.5 fusion.13
  92.2 5.1 fusion.3
  97.3 4.1 fusion.1
  101.4 2.0 fusion.14
  105.7 1.8 add_multiply_fusion
  109.1 1.9 copy.122
  110.9 3.1 copy.123
  114.1 2.2 add_convert_fusion
  117.9 5.7 add_convert_fusion.4
  124.5 3.5 convert_add_fusion
  129.4 551.4 %all-reduce.3.cloned.1.call-done = (f32[1024,32]{0,1:T(8,128)}, f32[32,4096]{1,0:T(8,128)}) async-done(((f32[1024,32]{0,1:T(8,128)}, f32[32,4096]{1,0:T(8,128)}), (f32[1024,32]{0,1:T(8,128)}, f32[32,4096]{1,0:T(8,128)})) %all-reduce.3.cloned.1.call-update) | async-done | bytes 655376 | tf_op jit(solution)/shard_map/psum | solution.py:123
  680.8 1.9 broadcast_multiply_fusion
  (97 shorter events, 26.1 us)
Async XLA Ops:
  7.2 23.2 %copy-start = (bf16[32,4096]{1,0:T(8,128)(2,1)S(1)}, bf16[32,4096]{1,0:T(8,128)(2,1)}, u32[]{:S(2)}) copy-start(bf16[32,4096]{1,0:T(8,128)(2,1)} %param.15) | copy-start | bytes 786436
  7.2 6.0 copy-start.15
  7.2 8.4 %copy-start.12 = (bf16[512,1024]{1,0:T(8,128)(2,1)S(1)}, bf16[512,1024]{1,0:T(8,128)(2,1)}, u32[]{:S(2)}) copy-start(bf16[512,1024]{1,0:T(8,128)(2,1)} %param.9) | copy-start | bytes 3145732
  7.2 673.6 %all-reduce.3.cloned.1.call-start = ((), (), s32[]{:S(2)}) async-start(), calls=%async_computation | async-start | bytes 1310720 | tf_op jit(solution)/shard_map/psum | solution.py:123
  10.6 10.2 %copy-start.4 = (f32[512,64]{1,0:T(8,128)}, f32[512,64]{1,0:T(8,128)S(1)}, u32[]{:S(2)}) copy-start(f32[512,64]{1,0:T(8,128)S(1)} %get-tuple-element.31) | copy-start | bytes 393220
  10.6 10.2 %copy-start.7 = (f32[512,64]{1,0:T(8,128)}, f32[512,64]{1,0:T(8,128)S(1)}, u32[]{:S(2)}) copy-start(f32[512,64]{1,0:T(8,128)S(1)} %get-tuple-element.32) | copy-start | bytes 393220
  11.6 35.0 %collective-permute-start = (bf16[512,2,128]{2,0,1:T(8,128)(2,1)}, bf16[512,2,128]{2,0,1:T(8,128)(2,1)}, u32[]{:S(2)}, u32[]{:S(2)}) collective-permute-start(bf16[512,2,128]{2,0,1:T(8,128)(2,1)} %pad_maximum_fusion.1), channel_id=1, source_target_pairs={{0,4},{4,8},{8,12},{12,16},{16,20},{20,24},{24,28},{28,32},{32,36}... | collective-permute-start | bytes 786440 | tf_op jit(solution)/shard_map/ppermute | solution.py:11
  14.1 43.6 %collective-permute-start.1 = (bf16[512,2,128]{0,2,1:T(8,128)(2,1)}, bf16[512,2,128]{0,2,1:T(8,128)(2,1)}, u32[]{:S(2)}, u32[]{:S(2)}) collective-permute-start(bf16[512,2,128]{0,2,1:T(8,128)(2,1)} %bitcast.14), channel_id=1, source_target_pairs={{0,4},{4,8},{8,12},{12,16},{16,20},{20,24},{24,28},{28,32},{32,36}... | collective-permute-start | bytes 786440 | tf_op jit(solution)/shard_map/ppermute | solution.py:11
  30.4 12.7 %slice-start = ((s8[8388608]{0:T(1024)(128)(4,1)}), s8[4194304]{0:T(1024)(128)(4,1)S(1)}, s32[]{:S(2)}) async-start(s8[8388608]{0:T(1024)(128)(4,1)} %bitcast.187), calls=%async_computation.1 | async-start | bytes 8388608
  34.0 9.0 %slice-start.1 = ((s8[8388608]{0:T(1024)(128)(4,1)}), s8[4194304]{0:T(1024)(128)(4,1)S(1)}, s32[]{:S(2)}) async-start(s8[8388608]{0:T(1024)(128)(4,1)} %bitcast.187), calls=%async_computation.2 | async-start | bytes 8388608
  34.1 9.0 %copy-start.10 = (pred[512,512]{0,1:T(8,128)(4,1)S(1)}, pred[512,512]{0,1:T(8,128)(4,1)}, u32[]{:S(2)}) copy-start(pred[512,512]{0,1:T(8,128)(4,1)} %copy.50) | copy-start | bytes 786436
  49.0 8.7 %copy-start.2 = (f32[2,512,512,4]{2,1,3,0:T(8,128)}, f32[2,512,512,4]{2,1,3,0:T(8,128)S(1)}, u32[]{:S(2)}) copy-start(f32[2,512,512,4]{2,1,3,0:T(8,128)S(1)} %get-tuple-element.39) | copy-start | bytes 25165828
  50.8 6.8 copy-start.13
  85.2 12.1 %slice-start.2 = ((s8[8388608]{0:T(1024)(128)(4,1)}), s8[4194304]{0:T(1024)(128)(4,1)S(1)}, s32[]{:S(2)}) async-start(s8[8388608]{0:T(1024)(128)(4,1)} %bitcast.189), calls=%async_computation.3 | async-start | bytes 8388608
  91.7 26.2 %collective-permute-start.3 = (bf16[512,2,128]{0,2,1:T(8,128)(2,1)}, bf16[512,2,128]{0,2,1:T(8,128)(2,1)}, u32[]{:S(2)}, u32[]{:S(2)}) collective-permute-start(bf16[512,2,128]{0,2,1:T(8,128)(2,1)} %fusion.13), channel_id=1, source_target_pairs={{0,252},{4,0},{8,4},{12,8},{16,12},{20,16},{24,20},{28,24},{32,28}... | collective-permute-start | bytes 786440 | tf_op jit(solution)/shard_map/ppermute | solution.py:11
  92.2 5.1 slice-start.3
  97.3 6.7 copy-start.3
  103.3 21.2 %collective-permute-start.2 = (bf16[512,2,128]{2,0,1:T(8,128)(2,1)}, bf16[512,2,128]{2,0,1:T(8,128)(2,1)}, u32[]{:S(2)}, u32[]{:S(2)}) collective-permute-start(bf16[512,2,128]{2,0,1:T(8,128)(2,1)} %fusion.14), channel_id=1, source_target_pairs={{0,252},{4,0},{8,4},{12,8},{16,12},{20,16},{24,20},{28,24},{32,28}... | collective-permute-start | bytes 786440 | tf_op jit(solution)/shard_map/ppermute | solution.py:11
  109.1 5.0 copy-start.5
  114.1 3.8 copy-start.11
  114.1 3.8 copy-start.14
  123.6 4.3 copy-start.6
  123.6 4.3 copy-start.8
  123.6 560.6 %copy-start.1 = (bf16[32,4096]{1,0:T(8,128)(2,1)S(1)}, bf16[32,4096]{1,0:T(8,128)(2,1)}, u32[]{:S(2)}) copy-start(bf16[32,4096]{1,0:T(8,128)(2,1)} %param.15) | copy-start | bytes 786436
  (4 other events, 9.8 us)
Sparse Core Ops, SparseCore 0:
  114.2 566.5 all-reduce.2
where the time goes:
time: 705 us; the launch traced here: 691 us
  waiting for transfers between devices  551 us (78%)
  matrix products  67.2 us (10%)
  blocking collectives  18.5 us (3%)
  local copies, waits for them, and re-layouts  17.6 us (2%)
  other arithmetic  17.6 us (2%)
  between operations  14.8 us (2%)
    psum x1, waiting for transfers between devices, shards(): down_factor_sum, up_factor_sum = lax.psum((a_term, b_term), 'seq')  551 us
    psum x1, blocking collectives, shards(): lax.psum(jnp.dot(attention_output, adapter_down, preferred_element_type=j...  18.5 us
  transfers between devices with their start and end apart: 5, of which 1 were waited for; matrix products, arithmetic and copies ran while one was open for 11% of the time, Pallas kernels for 0%

commit v1 on v0

v1 whole, which is shorter than its diff:
```python
import jax
import jax.numpy as jnp
from jax import lax
from jax.experimental import pallas as pl
from jax.experimental.pallas import tpu as pltpu
from jax.sharding import PartitionSpec as P

HEAD = 128
ROWS = 512
HALF = 256
HEADS = 8
WIDTH = 4096
MESH = pl.DeviceIdType.MESH
F32 = jnp.float32
BF16 = jnp.bfloat16
SCALE = HEAD**-0.5
LOG2E = 1.4426950408889634
HIDDEN = -1e30

K_NEXT, V_NEXT, MID, RS1A, RS1B, RS2, AG1, AG2, AG3, BACK, COPIES = 0, 1, 2, 6, 14, 22, 30, 38, 46, 50, 52


def dot(a, b):
    return jnp.dot(a, b, preferred_element_type=F32)


def dot_nt(a, b):
    return lax.dot_general(a, b, (((1,), (1,)), ((), ())), preferred_element_type=F32)


def seq_at(j, z):
    return (j // 4) * 32 + z * 4 + j % 4


def layer_kernel(
    q_hbm, k_in, v_in, og_hbm, w_hbm, down_t, up_in, cos_t, sin_t, pos_row, codes,
    dq_out, dk_out, dv_out, a_out, b_out,
    q_nat, og, w, k_all, v_all, k_t, v_t, q_t, diag, weights, attn_t, d_attn_t, back_t, down,
    dk_acc, dv_acc, mid_own, mid_all, back_send, back_recv,
    part_a, part_b, rs1a, rs1b, red1, rs2, ag1, full, b_all,
    load_sem, send_sem, recv_sem,
):
    s, r = lax.axis_index("seq"), lax.axis_index("rep")
    z, j = (s // 4) % 8, (s // 32) * 4 + s % 4
    along_z = [(seq_at(j, (z + o) % 8), r) for o in range(8)]
    along_j = [(seq_at((j + o) % 8, z), r) for o in range(8)]
    along_r = [(s, (r + o) % 4) for o in range(4)]
    after, before = ((s + 1) % 64, r), ((s + 63) % 64, r)
    peers = along_z[1:] + along_j[1:] + along_r[1:] + [after, before]

    def remote(at, src, dst, device):
        return pltpu.make_async_remote_copy(
            src_ref=src, dst_ref=dst, send_sem=send_sem.at[at], recv_sem=recv_sem.at[at],
            device_id=device, device_id_type=MESH,
        )

    def k_next():
        return remote(K_NEXT, k_all.at[:, 0:ROWS], k_all.at[:, ROWS : 2 * ROWS], after)

    def v_next():
        return remote(V_NEXT, v_all.at[:, 0:ROWS], v_all.at[:, ROWS : 2 * ROWS], after)

    def mids():
        return [remote(MID + o, mid_own, mid_all.at[o], along_r[o]) for o in range(1, 4)]

    def rs1_a():
        return [
            remote(RS1A + o, part_a.at[(z + o) % 8], rs1a.at[o], along_z[o]) for o in range(1, 8)
        ]

    def rs1_b():
        return [
            remote(RS1B + o, part_b.at[(z + o) % 8], rs1b.at[o], along_z[o]) for o in range(1, 8)
        ]

    def rs2_all():
        return [remote(RS2 + o, red1.at[(j + o) % 8], rs2.at[o], along_j[o]) for o in range(1, 8)]

    def ag1_all():
        return [remote(AG1 + o, ag1.at[j], ag1.at[j], along_j[o]) for o in range(1, 8)]

    def ag2_all():
        return [remote(AG2 + o, full.at[z], full.at[z], along_z[o]) for o in range(1, 8)]

    def ag3_all():
        return [remote(AG3 + o, b_all.at[r], b_all.at[r], along_r[o]) for o in range(1, 4)]

    def back_copy(g):
        return remote(BACK + g, back_send.at[g], back_recv.at[g], before)

    def begin(copies):
        for copy in copies:
            copy.start()

    def finish(copies):
        for copy in copies:
            copy.wait()

    barrier = pltpu.get_barrier_semaphore()
    for p in peers:
        pl.semaphore_signal(barrier, inc=1, device_id=p, device_id_type=MESH)
    load_q = pltpu.make_async_copy(q_hbm, q_nat, load_sem.at[0])
    load_og = pltpu.make_async_copy(og_hbm, og, load_sem.at[1])
    load_w = pltpu.make_async_copy(w_hbm, w, load_sem.at[2])
    load_q.start()
    load_og.start()
    load_w.start()

    cosine, sine = cos_t[...], sin_t[...]

    def turned(x):
        x1, x2 = x[:64], x[64:]
        return jnp.concatenate([x1 * cosine - x2 * sine, x2 * cosine + x1 * sine], 0)

    for g in range(2):
        v_own = v_in[:, g * HEAD : (g + 1) * HEAD]
        v_all[g, 0:ROWS] = v_own
        v_t[g, :, 0:ROWS] = v_own.astype(F32).T.astype(BF16)
        k_turned = turned(k_in[:, g * HEAD : (g + 1) * HEAD].astype(F32).T)
        k_t[g, :, 0:ROWS] = k_turned.astype(BF16)
        k_all[g, 0:ROWS] = k_turned.T.astype(BF16)
    pl.semaphore_wait(barrier, len(peers))
    k_next().start()
    v_next().start()

    q_pos = pos_row[...]
    k_pos = jnp.broadcast_to(q_pos, (8, ROWS)).T[:, 0:1]

    def hidden(step, a, b):
        return jnp.where(codes[step * 4 + a * 2 + b] == 1, 0.0, HIDDEN).astype(F32)

    for a in range(2):
        code = codes[a * 3]
        early = k_pos[a * HALF : (a + 1) * HALF] <= q_pos[:, a * HALF : (a + 1) * HALF]
        shown = jnp.where(early, jnp.where(code >= 1, 0.0, HIDDEN), jnp.where(code == 1, 0.0, HIDDEN))
        diag[a] = shown.astype(F32)

    down[...] = down_t[...].astype(F32).T.astype(BF16)
    dk_acc[...] = jnp.zeros_like(dk_acc)
    dv_acc[...] = jnp.zeros_like(dv_acc)

    load_q.wait()

    def turn_queries(h, carry):
        x = q_nat[:, pl.ds(pl.multiple_of(h * HEAD, HEAD), HEAD)].astype(F32).T
        q_t[h] = turned(x).astype(BF16)
        return carry

    lax.fori_loop(0, HEADS, turn_queries, 0)

    load_og.wait()
    back_t[...] = dot_nt(up_in[...], og[...]).astype(BF16)

    k_next().wait()
    v_next().wait()
    for g in range(2):
        k_t[g, :, ROWS : 2 * ROWS] = k_all[g, ROWS : 2 * ROWS].astype(F32).T.astype(BF16)
        v_t[g, :, ROWS : 2 * ROWS] = v_all[g, ROWS : 2 * ROWS].astype(F32).T.astype(BF16)

    def forward(h, carry):
        g = h // 4
        for a in range(2):
            cols = slice(a * HALF, (a + 1) * HALF)
            raw = dot(k_all[g], q_t[h, :, cols])
            blocks = []
            for i in range(4):
                block = raw[i * HALF : (i + 1) * HALF]
                if i == a:
                    block = block + diag[a]
                    blocks.append((block, None, jnp.max(block, 0, keepdims=True)))
                else:
                    off = hidden(i // 2, a, i % 2)
                    blocks.append((block, off, jnp.max(block, 0, keepdims=True) + off))
            top = jnp.maximum(
                jnp.maximum(blocks[0][2], blocks[1][2]), jnp.maximum(blocks[2][2], blocks[3][2])
            )
            shift = top * (-SCALE * LOG2E)
            total = jnp.zeros((1, HALF), F32)
            powers = []
            for block, off, _ in blocks:
                e = jnp.exp2(block * (SCALE * LOG2E) + (shift if off is None else shift + off))
                total = total + jnp.sum(e, 0, keepdims=True)
                powers.append(e)
            share = 1.0 / total
            for i in range(4):
                weights[h, i * HALF : (i + 1) * HALF, cols] = (powers[i] * share).astype(BF16)
            attn_t[h, :, cols] = dot(v_t[g], weights[h, :, cols]).astype(BF16)
        return carry

    lax.fori_loop(0, HEADS, forward, 0)

    mid_part = dot(down_t[...], attn_t[...].reshape(HEADS * HEAD, ROWS))
    mid_own[...] = mid_part.astype(BF16)
    begin(mids())
    for h in range(HEADS):
        part_a[h] = dot_nt(back_t[...], attn_t[h])
    begin(rs1_a())

    load_w.wait()

    def project(i, carry):
        at = pl.multiple_of(i * 512, 512)
        x = dot_nt(w[pl.ds(at, 512)], og[...]) + 2.0 * dot(down[pl.ds(at, 512)], back_t[...])
        d_attn_t[pl.ds(i * 4, 4)] = x.astype(BF16).reshape(4, HEAD, ROWS)
        return carry

    lax.fori_loop(0, 2, project, 0)

    finish(mids())
    mid = mid_part
    for o in range(1, 4):
        mid = mid + mid_all[o].astype(F32)
    b_part = dot(mid.astype(BF16), og[:, pl.ds(pl.multiple_of(r * 1024, 1024), 1024)])
    for c in range(8):
        part_b[c] = b_part[:, c * HEAD : (c + 1) * HEAD]
    begin(rs1_b())

    def finish_keys(g):
        back_copy(g).wait()
        dk = dk_acc[g, 0:ROWS] * SCALE + back_recv[g, 0].astype(F32)
        x = dk.T
        x1, x2 = x[:64], x[64:]
        x = jnp.concatenate([x1 * cosine + x2 * sine, x2 * cosine - x1 * sine], 0)
        dk_out[:, g * HEAD : (g + 1) * HEAD] = x.T.astype(BF16)
        dv = dv_acc[g, 0:ROWS] + back_recv[g, 1].astype(F32)
        dv_out[:, g * HEAD : (g + 1) * HEAD] = dv.astype(BF16)

    def send_back(g):
        back_send[g, 0] = (dk_acc[g, ROWS : 2 * ROWS] * SCALE).astype(BF16)
        back_send[g, 1] = dv_acc[g, ROWS : 2 * ROWS].astype(BF16)
        back_copy(g).start()

    def backward(h, carry):
        g = h // 4

        @pl.when(h == 2)
        def _():
            finish(rs1_a())
            finish(rs1_b())
            total_a, total_b = part_a[z], part_b[z]
            for o in range(1, 8):
                total_a = total_a + rs1a[o]
                total_b = total_b + rs1b[o]
            red1[0:4] = total_a.reshape(4, 8, HEAD)
            red1[4:8] = total_b.reshape(4, 8, HEAD)
            begin(rs2_all())

        @pl.when(h == 4)
        def _():
            send_back(0)
            finish(rs2_all())
            total = red1[j]
            for o in range(1, 8):
                total = total + rs2[o]
            ag1[j] = 2.0 * total
            begin(ag1_all())

        @pl.when(h == 6)
        def _():
            finish(ag1_all())
            full[z] = ag1[...].reshape(64, HEAD)
            begin(ag2_all())

        for a in range(2):
            cols = slice(a * HALF, (a + 1) * HALF)
            grad = d_attn_t[h, :, cols]
            delta = jnp.sum(grad.astype(F32) * attn_t[h, :, cols].astype(F32), 0, keepdims=True)
            p = weights[h, :, cols]
            d_score = (p.astype(F32) * (dot(v_all[g], grad) - delta)).astype(BF16)
            dq = dot(k_t[g], d_score) * SCALE
            x1, x2 = dq[:64], dq[64:]
            c, n = cosine[:, cols], sine[:, cols]
            x = jnp.concatenate([x1 * c + x2 * n, x2 * c - x1 * n], 0)
            dq_out[cols, pl.ds(pl.multiple_of(h * HEAD, HEAD), HEAD)] = x.T.astype(BF16)
            dk_acc[g] += dot_nt(d_score, q_t[h, :, cols])
            dv_acc[g] += dot_nt(p, grad)
        return carry

    lax.fori_loop(0, HEADS, backward, 0)
    send_back(1)

    finish(ag2_all())
    b_all[r] = full[:, 32:64, :]
    begin(ag3_all())
    finish_keys(0)
    for c in range(8):
        a_out[:, c * HEAD : (c + 1) * HEAD] = full[c, 0:32, :]
    finish_keys(1)
    finish(ag3_all())
    for p in range(4):
        for c in range(8):
            at = p * 1024 + c * HEAD
            b_out[:, at : at + HEAD] = b_all[p, c]


def shards(
    queries,
    keys,
    values,
    output_gradient,
    output_weight,
    adapter_down,
    adapter_up,
    positions,
    block_pair_mask,
):
    freq = 1000000.0 ** (-(jnp.arange(HEAD // 2).astype(F32) * 2.0 / HEAD))
    pos = positions.astype(F32)
    phase = freq[:, None] * pos[None, :]
    vmem = pl.BlockSpec(memory_space=pltpu.VMEM)
    smem = pl.BlockSpec(memory_space=pltpu.SMEM)
    hbm = pl.BlockSpec(memory_space=pl.ANY)
    out = jax.ShapeDtypeStruct
    dq, dk, dv, a, b = pl.pallas_call(
        layer_kernel,
        out_shape=(
            out((ROWS, HEADS * HEAD), BF16),
            out((ROWS, 2 * HEAD), BF16),
            out((ROWS, 2 * HEAD), BF16),
            out((32, HEADS * HEAD), F32),
            out((32, WIDTH), F32),
        ),
        in_specs=[hbm, vmem, vmem, hbm, hbm, vmem, vmem, vmem, vmem, vmem, smem],
        out_specs=(vmem,) * 5,
        scratch_shapes=[
            pltpu.VMEM((ROWS, HEADS * HEAD), BF16),
            pltpu.VMEM((ROWS, WIDTH), BF16),
            pltpu.VMEM((HEADS * HEAD, WIDTH), BF16),
            pltpu.VMEM((2, 2 * ROWS, HEAD), BF16),
            pltpu.VMEM((2, 2 * ROWS, HEAD), BF16),
            pltpu.VMEM((2, HEAD, 2 * ROWS), BF16),
            pltpu.VMEM((2, HEAD, 2 * ROWS), BF16),
            pltpu.VMEM((HEADS, HEAD, ROWS), BF16),
            pltpu.VMEM((2, HALF, HALF), F32),
            pltpu.VMEM((HEADS, 2 * ROWS, ROWS), BF16),
            pltpu.VMEM((HEADS, HEAD, ROWS), BF16),
            pltpu.VMEM((HEADS, HEAD, ROWS), BF16),
            pltpu.VMEM((32, ROWS), BF16),
            pltpu.VMEM((HEADS * HEAD, 32), BF16),
            pltpu.VMEM((2, 2 * ROWS, HEAD), F32),
            pltpu.VMEM((2, 2 * ROWS, HEAD), F32),
            pltpu.VMEM((32, ROWS), BF16),
            pltpu.VMEM((4, 32, ROWS), BF16),
            pltpu.VMEM((2, 2, ROWS, HEAD), BF16),
            pltpu.VMEM((2, 2, ROWS, HEAD), BF16),
            pltpu.VMEM((8, 32, HEAD), F32),
            pltpu.VMEM((8, 32, HEAD), F32),
            pltpu.VMEM((8, 32, HEAD), F32),
            pltpu.VMEM((8, 32, HEAD), F32),
            pltpu.VMEM((8, 8, HEAD), F32),
            pltpu.VMEM((8, 8, HEAD), F32),
            pltpu.VMEM((8, 8, HEAD), F32),
            pltpu.VMEM((8, 64, HEAD), F32),
            pltpu.VMEM((4, 8, 32, HEAD), F32),
            pltpu.SemaphoreType.DMA((3,)),
            pltpu.SemaphoreType.DMA((COPIES,)),
            pltpu.SemaphoreType.DMA((COPIES,)),
        ],
        compiler_params=pltpu.CompilerParams(
            collective_id=0, has_side_effects=True, vmem_limit_bytes=56 * 1024 * 1024
        ),
    )(
        queries,
        keys,
        values,
        output_gradient,
        output_weight,
        adapter_down.T,
        adapter_up,
        jnp.cos(phase),
        jnp.sin(phase),
        pos[None, :],
        block_pair_mask.reshape(8),
    )
    return dq, dk, dv, a.T, b


def solution(mesh):
    placed = (
        P("seq", "rep"),
        P("seq", "rep"),
        P("seq", "rep"),
        P("seq", None),
        P("rep", None),
        P("rep", None),
        P(),
        P("seq"),
        P("seq", None, None, None),
    )
    return jax.shard_map(
        shards,
        mesh=mesh,
        in_specs=placed,
        out_specs=(P("seq", "rep"), P("seq", "rep"), P("seq", "rep"), P("rep", None), P()),
        check_vma=False,
    )
```

time: 705 us -> 91 us (0.13)
  the two profiles are of different devices: /device:TPU:24 before, /device:TPU:1 now
where the time goes in v1:
time: 91 us; the launch traced here: 90.7 us
  Pallas kernels  77.8 us (85%)
  local copies, waits for them, and re-layouts  10.3 us (11%)
  other arithmetic  1.93 us (2%)
    pallas_call x1, Pallas kernels, shards(): pl.pallas_call(layer_kernel, out_shape=(out((ROWS, HEADS * HEAD), BF16),...  77.8 us
    unnamed x7, local copies, waits for them, and re-layouts  9.04 us

profile of v1, /device:TPU:1, one launch (start us, length us, event | category | flops | bytes accessed | tf_op | source)
XLA Modules:
  0.0 90.7 jit_solution(13829092006807200771)
XLA Ops:
  0.6 1.3 %reshape.21.codes = s32[8]{0:T(128)} reshape(s32[1,2,2,2]{3,2,1,0:T(2,128)} %param.17) | data formatting | bytes 64 | tf_op jit(solution)/shard_map/reshape | solution.py:373
  1.9 0.7 convert_element_type.11
  2.6 0.0 copy-start
  2.6 1.2 %multiply_sine_fusion = (f32[64,512]{1,0:T(8,128)}, f32[64,512]{1,0:T(8,128)}) fusion(f32[512]{0:T(512)S(1)} %convert_element_type.11, f32[64]{0:T(128)S(1)} %negate_power_fusion), kind=kLoop, calls=%fused_computation | loop fusion | flops 32768 | bytes 264448 | tf_op jit(solution)/shard_map/sin | solution.py:371
  3.8 0.0 copy-done
  3.8 77.8 %shard_map.128 = (bf16[512,1024]{1,0:T(8,128)(2,1)}, bf16[512,256]{1,0:T(8,128)(2,1)}, bf16[512,256]{1,0:T(8,128)(2,1)}, f32[32,1024]{1,0:T(8,128)}, f32[32,4096]{1,0:T(8,128)}) custom-call(bf16[512,1024]{1,0:T(8,128)(2,1)} %q_hbm.1, bf16[512,256]{1,0:T(8,128)(2,1)} %k_in.1, bf16[512,256]{1,0:T(8,128)(2,1)} %v_in.1, bf16[512,4096]{1,0:T(8,128)(2,1)} %og_hbm.1, ...), custom_call_target="tpu_custom_call" | custom-call | tf_op jit(solution)/shard_map/pallas_call | solution.py:314
  81.7 2.3 %copy.19 = bf16[512,1024]{1,0:T(8,128)(2,1)} copy(bf16[512,1024]{1,0:T(8,128)(2,1)} %get-tuple-element.22) | data formatting | bytes 2097152
  84.0 1.7 %copy.20 = bf16[512,256]{1,0:T(8,128)(2,1)} copy(bf16[512,256]{1,0:T(8,128)(2,1)} %get-tuple-element.23) | data formatting | bytes 524288
  85.6 1.7 %copy.21 = bf16[512,256]{1,0:T(8,128)(2,1)} copy(bf16[512,256]{1,0:T(8,128)(2,1)} %get-tuple-element.24) | data formatting | bytes 524288
  87.3 1.6 %copy.22 = f32[1024,32]{0,1:T(8,128)} copy(f32[1024,32]{0,1:T(8,128)} %bitcast.3) | data formatting | bytes 262144
  88.9 1.9 %copy.23 = f32[32,4096]{1,0:T(8,128)} copy(f32[32,4096]{1,0:T(8,128)} %get-tuple-element.26) | data formatting | bytes 1048576
  (1 shorter events, 0.0 us)
Async XLA Ops:
  2.6 1.2 %copy-start = (f32[512]{0:T(512)}, f32[512]{0:T(512)S(1)}, u32[]{:S(2)}) copy-start(f32[512]{0:T(512)S(1)} %convert_element_type.11) | copy-start | bytes 6148

commit v2 on v1

--- a/solution.py
+++ b/solution.py
@@ -14,10 +14,10 @@
 F32 = jnp.float32
 BF16 = jnp.bfloat16
 SCALE = HEAD**-0.5
-LOG2E = 1.4426950408889634
+POWER = SCALE * 1.4426950408889634
 HIDDEN = -1e30
 
-K_NEXT, V_NEXT, MID, RS1A, RS1B, RS2, AG1, AG2, AG3, BACK, COPIES = 0, 1, 2, 6, 14, 22, 30, 38, 46, 50, 52
+K_NEXT, V_NEXT, MID, RS1A, RS1B, ALLJ, AG2, BACK, AG3, COPIES = 0, 2, 4, 8, 16, 24, 32, 40, 42, 74
 
 
 def dot(a, b):
@@ -35,9 +35,9 @@
 def layer_kernel(
     q_hbm, k_in, v_in, og_hbm, w_hbm, down_t, up_in, cos_t, sin_t, pos_row, codes,
     dq_out, dk_out, dv_out, a_out, b_out,
-    q_nat, og, w, k_all, v_all, k_t, v_t, q_t, diag, weights, attn_t, d_attn_t, back_t, down,
+    q_nat, og, w, k_all, v_all, k_t, v_t, q_t, diag, weights, stats, attn_own, attn_t, d_attn_t, back_t, down,
     dk_acc, dv_acc, mid_own, mid_all, back_send, back_recv,
-    part_a, part_b, rs1a, rs1b, red1, rs2, ag1, full, b_all,
+    part_a, part_b, rs1a, rs1b, all_j, full, b_all,
     load_sem, send_sem, recv_sem,
 ):
     s, r = lax.axis_index("seq"), lax.axis_index("rep")
@@ -54,11 +54,11 @@
             device_id=device, device_id_type=MESH,
         )
 
-    def k_next():
-        return remote(K_NEXT, k_all.at[:, 0:ROWS], k_all.at[:, ROWS : 2 * ROWS], after)
-
-    def v_next():
-        return remote(V_NEXT, v_all.at[:, 0:ROWS], v_all.at[:, ROWS : 2 * ROWS], after)
+    def next_copies(g):
+        return [
+            remote(K_NEXT + g, k_all.at[g, 0:ROWS], k_all.at[g, ROWS : 2 * ROWS], after),
+            remote(V_NEXT + g, v_all.at[g, 0:ROWS], v_all.at[g, ROWS : 2 * ROWS], after),
+        ]
 
     def mids():
         return [remote(MID + o, mid_own, mid_all.at[o], along_r[o]) for o in range(1, 4)]
@@ -73,17 +73,16 @@
             remote(RS1B + o, part_b.at[(z + o) % 8], rs1b.at[o], along_z[o]) for o in range(1, 8)
         ]
 
-    def rs2_all():
-        return [remote(RS2 + o, red1.at[(j + o) % 8], rs2.at[o], along_j[o]) for o in range(1, 8)]
-
-    def ag1_all():
-        return [remote(AG1 + o, ag1.at[j], ag1.at[j], along_j[o]) for o in range(1, 8)]
-
-    def ag2_all():
-        return [remote(AG2 + o, full.at[z], full.at[z], along_z[o]) for o in range(1, 8)]
-
-    def ag3_all():
-        return [remote(AG3 + o, b_all.at[r], b_all.at[r], along_r[o]) for o in range(1, 4)]
+    def all_j_copies():
+        return [remote(ALLJ + o, all_j.at[j], all_j.at[j], along_j[o]) for o in range(1, 8)]
+
+    def ag2(o):
+        return remote(AG2 + o, full.at[z], full.at[z], along_z[o])
+
+    def ag3(k):
+        block = full.at[(z + 8 - k) % 8, 32:64]
+        land = b_all.at[r, (z + 8 - k) % 8]
+        return [remote(AG3 + k * 4 + o, block, land, along_r[o]) for o in range(1, 4)]
 
     def back_copy(g):
         return remote(BACK + g, back_send.at[g], back_recv.at[g], before)
@@ -119,18 +118,15 @@
         k_turned = turned(k_in[:, g * HEAD : (g + 1) * HEAD].astype(F32).T)
         k_t[g, :, 0:ROWS] = k_turned.astype(BF16)
         k_all[g, 0:ROWS] = k_turned.T.astype(BF16)
-    pl.semaphore_wait(barrier, len(peers))
-    k_next().start()
-    v_next().start()
-
-    q_pos = pos_row[...]
+
+    q_pos = pos_row[...].astype(F32)
     k_pos = jnp.broadcast_to(q_pos, (8, ROWS)).T[:, 0:1]
 
     def hidden(step, a, b):
-        return jnp.where(codes[step * 4 + a * 2 + b] == 1, 0.0, HIDDEN).astype(F32)
+        return jnp.where(codes[0, step, a, b] == 1, 0.0, HIDDEN).astype(F32)
 
     for a in range(2):
-        code = codes[a * 3]
+        code = codes[0, 0, a, a]
         early = k_pos[a * HALF : (a + 1) * HALF] <= q_pos[:, a * HALF : (a + 1) * HALF]
         shown = jnp.where(early, jnp.where(code >= 1, 0.0, HIDDEN), jnp.where(code == 1, 0.0, HIDDEN))
         diag[a] = shown.astype(F32)
@@ -148,52 +144,93 @@
 
     lax.fori_loop(0, HEADS, turn_queries, 0)
 
-    load_og.wait()
-    back_t[...] = dot_nt(up_in[...], og[...]).astype(BF16)
-
-    k_next().wait()
-    v_next().wait()
-    for g in range(2):
+    pl.semaphore_wait(barrier, len(peers))
+    begin(next_copies(0))
+
+    def forward_own(h, carry):
+        g = h // 4
+
+        @pl.when(h == 4)
+        def _():
+            for copy in next_copies(0):
+                copy.wait_send()
+            begin(next_copies(1))
+
+        for a in range(2):
+            cols = slice(a * HALF, (a + 1) * HALF)
+            raw = dot(k_all[g, 0:ROWS], q_t[h, :, cols])
+            same = raw[a * HALF : (a + 1) * HALF] + diag[a]
+            other = raw[(1 - a) * HALF : (2 - a) * HALF]
+            off = hidden(0, a, 1 - a)
+            top = jnp.maximum(
+                jnp.max(same, 0, keepdims=True), jnp.max(other, 0, keepdims=True) + off
+            )
+            shift = top * -POWER
+            same = jnp.exp2(same * POWER + shift)
+            other = jnp.exp2(other * POWER + (shift + off))
+            weights[h, a * HALF : (a + 1) * HALF, cols] = same.astype(BF16)
+            weights[h, (1 - a) * HALF : (2 - a) * HALF, cols] = other.astype(BF16)
+            stats[h, 0:1, cols] = top
+            stats[h, 1:2, cols] = jnp.sum(same, 0, keepdims=True) + jnp.sum(other, 0, keepdims=True)
+            attn_own[h, :, cols] = dot(v_t[g, :, 0:ROWS], weights[h, 0:ROWS, cols])
+        return carry
+
+    lax.fori_loop(0, HEADS, forward_own, 0)
+
+    def take_previous(g):
+        for copy in next_copies(g):
+            copy.wait_recv()
         k_t[g, :, ROWS : 2 * ROWS] = k_all[g, ROWS : 2 * ROWS].astype(F32).T.astype(BF16)
         v_t[g, :, ROWS : 2 * ROWS] = v_all[g, ROWS : 2 * ROWS].astype(F32).T.astype(BF16)
 
-    def forward(h, carry):
+    def forward_previous(h, carry):
         g = h // 4
+
+        @pl.when(h == 0)
+        def _():
+            take_previous(0)
+
+        @pl.when(h == 4)
+        def _():
+            load_og.wait()
+            back_t[...] = dot_nt(up_in[...], og[...]).astype(BF16)
+            for copy in next_copies(1):
+                copy.wait_send()
+            take_previous(1)
+
         for a in range(2):
             cols = slice(a * HALF, (a + 1) * HALF)
-            raw = dot(k_all[g], q_t[h, :, cols])
-            blocks = []
-            for i in range(4):
-                block = raw[i * HALF : (i + 1) * HALF]
-                if i == a:
-                    block = block + diag[a]
-                    blocks.append((block, None, jnp.max(block, 0, keepdims=True)))
-                else:
-                    off = hidden(i // 2, a, i % 2)
-                    blocks.append((block, off, jnp.max(block, 0, keepdims=True) + off))
+            raw = dot(k_all[g, ROWS : 2 * ROWS], q_t[h, :, cols])
+            first, second = raw[0:HALF], raw[HALF:ROWS]
+            off1, off2 = hidden(1, a, 0), hidden(1, a, 1)
             top = jnp.maximum(
-                jnp.maximum(blocks[0][2], blocks[1][2]), jnp.maximum(blocks[2][2], blocks[3][2])
+                jnp.max(first, 0, keepdims=True) + off1, jnp.max(second, 0, keepdims=True) + off2
             )
-            shift = top * (-SCALE * LOG2E)
-            total = jnp.zeros((1, HALF), F32)
-            powers = []
-            for block, off, _ in blocks:
-                e = jnp.exp2(block * (SCALE * LOG2E) + (shift if off is None else shift + off))
-                total = total + jnp.sum(e, 0, keepdims=True)
-                powers.append(e)
-            share = 1.0 / total
-            for i in range(4):
-                weights[h, i * HALF : (i + 1) * HALF, cols] = (powers[i] * share).astype(BF16)
-            attn_t[h, :, cols] = dot(v_t[g], weights[h, :, cols]).astype(BF16)
+            shift = jnp.minimum(top * -POWER, 1e28)
+            first = jnp.exp2(first * POWER + (shift + off1))
+            second = jnp.exp2(second * POWER + (shift + off2))
+            weights[h, ROWS : ROWS + HALF, cols] = first.astype(BF16)
+            weights[h, ROWS + HALF : 2 * ROWS, cols] = second.astype(BF16)
+            total = jnp.sum(first, 0, keepdims=True) + jnp.sum(second, 0, keepdims=True)
+            top_own = stats[h, 0:1, cols]
+            top_all = jnp.maximum(top, top_own)
+            own = jnp.exp2((top_own - top_all) * POWER)
+            previous = jnp.exp2((top - top_all) * POWER)
+            share = 1.0 / (stats[h, 1:2, cols] * own + total * previous)
+            own, previous = own * share, previous * share
+            stats[h, 2:3, cols] = own
+            stats[h, 3:4, cols] = previous
+            part = dot(v_t[g, :, ROWS : 2 * ROWS], weights[h, ROWS : 2 * ROWS, cols])
+            attn_t[h, :, cols] = (attn_own[h, :, cols] * own + part * previous).astype(BF16)
         return carry
 
-    lax.fori_loop(0, HEADS, forward, 0)
+    lax.fori_loop(0, HEADS, forward_previous, 0)
 
     mid_part = dot(down_t[...], attn_t[...].reshape(HEADS * HEAD, ROWS))
     mid_own[...] = mid_part.astype(BF16)
     begin(mids())
     for h in range(HEADS):
-        part_a[h] = dot_nt(back_t[...], attn_t[h])
+        part_a[h] = dot_nt(back_t[...], attn_t[h]).astype(BF16)
     begin(rs1_a())
 
     load_w.wait()
@@ -212,7 +249,7 @@
         mid = mid + mid_all[o].astype(F32)
     b_part = dot(mid.astype(BF16), og[:, pl.ds(pl.multiple_of(r * 1024, 1024), 1024)])
     for c in range(8):
-        part_b[c] = b_part[:, c * HEAD : (c + 1) * HEAD]
+        part_b[c] = b_part[:, c * HEAD : (c + 1) * HEAD].astype(BF16)
     begin(rs1_b())
 
     def finish_keys(g):
@@ -237,60 +274,98 @@
         def _():
             finish(rs1_a())
             finish(rs1_b())
-            total_a, total_b = part_a[z], part_b[z]
+            total_a, total_b = part_a[z].astype(F32), part_b[z].astype(F32)
             for o in range(1, 8):
-                total_a = total_a + rs1a[o]
-                total_b = total_b + rs1b[o]
-            red1[0:4] = total_a.reshape(4, 8, HEAD)
-            red1[4:8] = total_b.reshape(4, 8, HEAD)
-            begin(rs2_all())
+                total_a = total_a + rs1a[o].astype(F32)
+                total_b = total_b + rs1b[o].astype(F32)
+            all_j[j, 0:32] = total_a
+            all_j[j, 32:64] = total_b
+            begin(all_j_copies())
 
         @pl.when(h == 4)
         def _():
             send_back(0)
-            finish(rs2_all())
-            total = red1[j]
+
+        @pl.when(h == 5)
+        def _():
+            finish(all_j_copies())
+            total = all_j[0]
             for o in range(1, 8):
-                total = total + rs2[o]
-            ag1[j] = 2.0 * total
-            begin(ag1_all())
-
-        @pl.when(h == 6)
-        def _():
-            finish(ag1_all())
-            full[z] = ag1[...].reshape(64, HEAD)
-            begin(ag2_all())
+                total = total + all_j[o]
+            full[z] = (2.0 * total).astype(BF16)
+            begin([ag2(o) for o in range(1, 8)])
+            begin(ag3(0))
+
+        @pl.when(h == 7)
+        def _():
+            for o in range(1, 8):
+                ag2(o).wait()
+                begin(ag3(o))
 
         for a in range(2):
             cols = slice(a * HALF, (a + 1) * HALF)
             grad = d_attn_t[h, :, cols]
             delta = jnp.sum(grad.astype(F32) * attn_t[h, :, cols].astype(F32), 0, keepdims=True)
-            p = weights[h, :, cols]
-            d_score = (p.astype(F32) * (dot(v_all[g], grad) - delta)).astype(BF16)
-            dq = dot(k_t[g], d_score) * SCALE
+            d_weight = dot(v_all[g], grad)
+            q_cols = q_t[h, :, cols]
+            dq = None
+            for t in range(2):
+                rows = slice(t * ROWS, (t + 1) * ROWS)
+                factor = stats[h, 2 + t : 3 + t, cols]
+                p = weights[h, rows, cols]
+                d_score = p.astype(F32) * (d_weight[rows] * factor - delta * factor)
+                d_score = d_score.astype(BF16)
+                part = dot(k_t[g, :, rows], d_score)
+                dq = part if dq is None else dq + part
+                dk_acc[g, rows] += dot_nt(d_score, q_cols)
+                dv_acc[g, rows] += dot_nt(p, (grad.astype(F32) * factor).astype(BF16))
+            dq = dq * SCALE
             x1, x2 = dq[:64], dq[64:]
             c, n = cosine[:, cols], sine[:, cols]
             x = jnp.concatenate([x1 * c + x2 * n, x2 * c - x1 * n], 0)
             dq_out[cols, pl.ds(pl.multiple_of(h * HEAD, HEAD), HEAD)] = x.T.astype(BF16)
-            dk_acc[g] += dot_nt(d_score, q_t[h, :, cols])
-            dv_acc[g] += dot_nt(p, grad)
         return carry
 
     lax.fori_loop(0, HEADS, backward, 0)
     send_back(1)
-
-    finish(ag2_all())
+    finish_keys(0)
     b_all[r] = full[:, 32:64, :]
-    begin(ag3_all())
-    finish_keys(0)
     for c in range(8):
-        a_out[:, c * HEAD : (c + 1) * HEAD] = full[c, 0:32, :]
+        a_out[:, c * HEAD : (c + 1) * HEAD] = full[c, 0:32].astype(F32)
     finish_keys(1)
-    finish(ag3_all())
+    for k in range(8):
+        finish(ag3(k))
+    b_out[...] = b_all[...]
+
+
+def write_kernel(
+    dq, dk, dv, a, b, dq_out, dk_out, dv_out, a_out, b_out,
+    dq_in, dk_in, dv_in, a_in, b_in, b_wide, in_sem, out_sem,
+):
+    quarter = ROWS // 4
+    steps = [(dk, dk_in, dk_out), (dv, dv_in, dv_out), (a, a_in, a_out)]
+    for i in range(4):
+        rows = slice(i * quarter, (i + 1) * quarter)
+        steps.append((dq.at[rows], dq_in.at[rows], dq_out.at[rows]))
+    loads = [pltpu.make_async_copy(x, y, in_sem.at[i]) for i, (x, y, _) in enumerate(steps)]
+    stores = [pltpu.make_async_copy(y, o, out_sem.at[i]) for i, (_, y, o) in enumerate(steps)]
+    load_b = pltpu.make_async_copy(b, b_in, in_sem.at[7])
+    store_b = pltpu.make_async_copy(b_wide, b_out, out_sem.at[7])
+    load_b.start()
+    for copy in loads:
+        copy.start()
+    load_b.wait()
     for p in range(4):
         for c in range(8):
             at = p * 1024 + c * HEAD
-            b_out[:, at : at + HEAD] = b_all[p, c]
+            b_wide[:, at : at + HEAD] = b_in[p, c].astype(F32)
+    store_b.start()
+    for load, store in zip(loads, stores):
+        load.wait()
+        store.start()
+    for copy in stores:
+        copy.wait()
+    store_b.wait()
 
 
 def shards(
@@ -305,8 +380,7 @@
     block_pair_mask,
 ):
     freq = 1000000.0 ** (-(jnp.arange(HEAD // 2).astype(F32) * 2.0 / HEAD))
-    pos = positions.astype(F32)
-    phase = freq[:, None] * pos[None, :]
+    phase = freq[:, None] * positions.astype(F32)[None, :]
     vmem = pl.BlockSpec(memory_space=pltpu.VMEM)
     smem = pl.BlockSpec(memory_space=pltpu.SMEM)
     hbm = pl.BlockSpec(memory_space=pl.ANY)
@@ -318,7 +392,7 @@
             out((ROWS, 2 * HEAD), BF16),
             out((ROWS, 2 * HEAD), BF16),
             out((32, HEADS * HEAD), F32),
-            out((32, WIDTH), F32),
+            out((4, 8, 32, HEAD), BF16),
         ),
         in_specs=[hbm, vmem, vmem, hbm, hbm, vmem, vmem, vmem, vmem, vmem, smem],
         out_specs=(vmem,) * 5,
@@ -333,6 +407,8 @@
             pltpu.VMEM((HEADS, HEAD, ROWS), BF16),
             pltpu.VMEM((2, HALF, HALF), F32),
             pltpu.VMEM((HEADS, 2 * ROWS, ROWS), BF16),
+            pltpu.VMEM((HEADS, 8, ROWS), F32),
+            pltpu.VMEM((HEADS, HEAD, ROWS), F32),
             pltpu.VMEM((HEADS, HEAD, ROWS), BF16),
             pltpu.VMEM((HEADS, HEAD, ROWS), BF16),
             pltpu.VMEM((32, ROWS), BF16),
@@ -343,15 +419,13 @@
             pltpu.VMEM((4, 32, ROWS), BF16),
             pltpu.VMEM((2, 2, ROWS, HEAD), BF16),
             pltpu.VMEM((2, 2, ROWS, HEAD), BF16),
-            pltpu.VMEM((8, 32, HEAD), F32),
-            pltpu.VMEM((8, 32, HEAD), F32),
-            pltpu.VMEM((8, 32, HEAD), F32),
-            pltpu.VMEM((8, 32, HEAD), F32),
-            pltpu.VMEM((8, 8, HEAD), F32),
-            pltpu.VMEM((8, 8, HEAD), F32),
-            pltpu.VMEM((8, 8, HEAD), F32),
+            pltpu.VMEM((8, 32, HEAD), BF16),
+            pltpu.VMEM((8, 32, HEAD), BF16),
+            pltpu.VMEM((8, 32, HEAD), BF16),
+            pltpu.VMEM((8, 32, HEAD), BF16),
             pltpu.VMEM((8, 64, HEAD), F32),
-            pltpu.VMEM((4, 8, 32, HEAD), F32),
+            pltpu.VMEM((8, 64, HEAD), BF16),
+            pltpu.VMEM((4, 8, 32, HEAD), BF16),
             pltpu.SemaphoreType.DMA((3,)),
             pltpu.SemaphoreType.DMA((COPIES,)),
             pltpu.SemaphoreType.DMA((COPIES,)),
@@ -369,9 +443,31 @@
         adapter_up,
         jnp.cos(phase),
         jnp.sin(phase),
-        pos[None, :],
-        block_pair_mask.reshape(8),
+        positions[None, :],
+        block_pair_mask,
     )
+    dq, dk, dv, a, b = pl.pallas_call(
+        write_kernel,
+        out_shape=(
+            out((ROWS, HEADS * HEAD), BF16),
+            out((ROWS, 2 * HEAD), BF16),
+            out((ROWS, 2 * HEAD), BF16),
+            out((32, HEADS * HEAD), F32),
+            out((32, WIDTH), F32),
+        ),
+        in_specs=[hbm] * 5,
+        out_specs=(hbm,) * 5,
+        scratch_shapes=[
+            pltpu.VMEM((ROWS, HEADS * HEAD), BF16),
+            pltpu.VMEM((ROWS, 2 * HEAD), BF16),
+            pltpu.VMEM((ROWS, 2 * HEAD), BF16),
+            pltpu.VMEM((32, HEADS * HEAD), F32),
+            pltpu.VMEM((4, 8, 32, HEAD), BF16),
+            pltpu.VMEM((32, WIDTH), F32),
+            pltpu.SemaphoreType.DMA((8,)),
+            pltpu.SemaphoreType.DMA((8,)),
+        ],
+    )(dq, dk, dv, a, b)
     return dq, dk, dv, a.T, b
 
 

time: 91 us -> 68.9 us (0.76)
  the two profiles are of different devices: /device:TPU:1 before, /device:TPU:24 now
where the time goes in v2:
time: 68.9 us; the launch traced here: 68.7 us
  Pallas kernels  66.2 us (96%)
  other arithmetic  1.93 us (3%)
    pallas_call x1, Pallas kernels, shards(): pl.pallas_call(layer_kernel, out_shape=(out((ROWS, HEADS * HEAD), BF16),...  63.7 us
    pallas_call x1, Pallas kernels, shards(): pl.pallas_call(write_kernel, out_shape=(out((ROWS, HEADS * HEAD), BF16),...  2.48 us

profile of v2, /device:TPU:24, one launch (start us, length us, event | category | flops | bytes accessed | tf_op | source)
XLA Modules:
  0.0 68.7 jit_solution(12090472115115451366)
XLA Ops:
  0.6 0.7 convert_element_type.11
  1.3 1.2 %multiply_sine_fusion = (f32[64,512]{1,0:T(8,128)}, f32[64,512]{1,0:T(8,128)}) fusion(f32[512]{0:T(512)S(1)} %convert_element_type.11, f32[64]{0:T(128)S(1)} %negate_power_fusion), kind=kLoop, calls=%fused_computation | loop fusion | flops 32768 | bytes 264448 | tf_op jit(solution)/shard_map/sin | solution.py:445
  2.6 63.7 %shard_map.128 = (bf16[512,1024]{1,0:T(8,128)(2,1)}, bf16[512,256]{1,0:T(8,128)(2,1)}, bf16[512,256]{1,0:T(8,128)(2,1)}, f32[32,1024]{1,0:T(8,128)}, bf16[4,8,32,128]{3,2,1,0:T(8,128)(2,1)}) custom-call(bf16[512,1024]{1,0:T(8,128)(2,1)} %q_hbm.1, bf16[512,256]{1,0:T(8,128)(2,1)} %k_in.1, bf16[512,256]{1,0:T(8,128)(2,1)} %v_in.1, bf16[512,4096]{1,0:T(8,128)(2,1)} %og_hbm.1, ...), custom_call_target="tpu_custom_call" | custom-call | tf_op jit(solution)/shard_map/pallas_call | solution.py:388
  66.3 2.5 %shard_map.129 = (bf16[512,1024]{1,0:T(8,128)(2,1)}, bf16[512,256]{1,0:T(8,128)(2,1)}, bf16[512,256]{1,0:T(8,128)(2,1)}, f32[32,1024]{1,0:T(8,128)}, f32[32,4096]{1,0:T(8,128)}) custom-call(bf16[512,1024]{1,0:T(8,128)(2,1)} %get-tuple-element.15.dq, bf16[512,256]{1,0:T(8,128)(2,1)} %get-tuple-element.16.dk, bf16[512,256]{1,0:T(8,128)(2,1)} %get-tuple-element.17.dv, ...), custom_call_target="tpu_custom_call" | custom-call | tf_op jit(solution)/shard_map/pallas_call | solution.py:449
  (1 shorter events, 0.0 us)

commit v3 on v2

v3 whole, which is shorter than its diff:
```python
import jax
import jax.numpy as jnp
import numpy as np
from jax import lax
from jax.experimental import pallas as pl
from jax.experimental.pallas import tpu as pltpu
from jax.sharding import PartitionSpec as P

HEAD = 128
ROWS = 512
HALF = 256
HEADS = 8
WIDTH = 4096
MESH = pl.DeviceIdType.MESH
F32 = jnp.float32
BF16 = jnp.bfloat16
SCALE = HEAD**-0.5
POWER = SCALE * 1.4426950408889634
HIDDEN = -1e30
AT_ONCE = 4
FREQUENCY = (1000000.0 ** (-np.arange(64) * 2.0 / 128)).astype(np.float32)

K_NEXT, V_NEXT, MID, RS1A, RS1B, ALLJ, AG2, BACK, AG3, COPIES = 0, 2, 4, 8, 16, 24, 32, 40, 42, 74


def dot(a, b):
    return jnp.dot(a, b, preferred_element_type=F32)


def dot_nt(a, b):
    return lax.dot_general(a, b, (((1,), (1,)), ((), ())), preferred_element_type=F32)


def seq_at(j, z):
    return (j // 4) * 32 + z * 4 + j % 4


def layer_kernel(
    q_hbm, k_hbm, v_hbm, og_hbm, w_hbm, down_hbm, up_hbm, freq, pos_row, codes,
    dq_hbm, dk_hbm, dv_hbm, a_hbm, b_out,
    k_nat, up, down_t, angle, dq_out, dk_out, dv_out, a_out,
    q_nat, og, w, k_all, v_all, k_t, v_t, q_t, diag, weights, stats, attn_own, attn_t, d_attn_t, back_t, down,
    dk_acc, dv_acc, mid_own, mid_all, back_send, back_recv,
    part_a, part_b, rs1a, rs1b, all_j, full, b_all,
    load_sem, store_sem, send_sem, recv_sem,
):
    s, r = lax.axis_index("seq"), lax.axis_index("rep")
    z, j = (s // 4) % 8, (s // 32) * 4 + s % 4
    along_z = [(seq_at(j, (z + o) % 8), r) for o in range(8)]
    along_j = [(seq_at((j + o) % 8, z), r) for o in range(8)]
    along_r = [(s, (r + o) % 4) for o in range(4)]
    after, before = ((s + 1) % 64, r), ((s + 63) % 64, r)
    peers = along_z[1:] + along_j[1:] + along_r[1:] + [after, before]

    def remote(at, src, dst, device):
        return pltpu.make_async_remote_copy(
            src_ref=src, dst_ref=dst, send_sem=send_sem.at[at], recv_sem=recv_sem.at[at],
            device_id=device, device_id_type=MESH,
        )

    def next_v(g):
        return remote(V_NEXT + g, v_all.at[g, 0:ROWS], v_all.at[g, ROWS : 2 * ROWS], after)

    def next_k(g):
        return remote(K_NEXT + g, k_all.at[g, 0:ROWS], k_all.at[g, ROWS : 2 * ROWS], after)

    def mids():
        return [remote(MID + o, mid_own, mid_all.at[o], along_r[o]) for o in range(1, 4)]

    def rs1_a():
        return [
            remote(RS1A + o, part_a.at[(z + o) % 8], rs1a.at[o], along_z[o]) for o in range(1, 8)
        ]

    def rs1_b():
        return [
            remote(RS1B + o, part_b.at[(z + o) % 8], rs1b.at[o], along_z[o]) for o in range(1, 8)
        ]

    def all_j_copies():
        return [remote(ALLJ + o, all_j.at[j], all_j.at[j], along_j[o]) for o in range(1, 8)]

    def ag2(o):
        return remote(AG2 + o, full.at[z], full.at[z], along_z[o])

    def ag3(k):
        block = full.at[(z + 8 - k) % 8, 32:64]
        land = b_all.at[r, (z + 8 - k) % 8]
        return [remote(AG3 + k * 4 + o, block, land, along_r[o]) for o in range(1, 4)]

    def back_copy(g):
        return remote(BACK + g, back_send.at[g], back_recv.at[g], before)

    def begin(copies):
        for copy in copies:
            copy.start()

    def finish(copies):
        for copy in copies:
            copy.wait()

    barrier = pltpu.get_barrier_semaphore()
    for p in peers:
        pl.semaphore_signal(barrier, inc=1, device_id=p, device_id_type=MESH)
    loads = []
    for at, (src, dst) in enumerate([
        (v_hbm.at[:, 0:HEAD], v_all.at[0, 0:ROWS]),
        (v_hbm.at[:, HEAD : 2 * HEAD], v_all.at[1, 0:ROWS]),
        (k_hbm, k_nat), (q_hbm, q_nat), (og_hbm, og), (up_hbm, up), (down_hbm, down_t), (w_hbm, w),
    ]):
        loads.append(pltpu.make_async_copy(src, dst, load_sem.at[at]))
        loads[at].start()
    load_v0, load_v1, load_k, load_q, load_og, load_up, load_down, load_w = loads

    load_v0.wait()
    pl.semaphore_wait(barrier, len(peers))
    next_v(0).start()
    q_pos = pos_row[...].astype(F32)
    phase = freq[:, 0:1] * q_pos
    angle[0] = jnp.cos(phase)
    angle[1] = jnp.sin(phase)
    cosine, sine = angle[0], angle[1]

    def turned(x):
        x1, x2 = x[:64], x[64:]
        return jnp.concatenate([x1 * cosine - x2 * sine, x2 * cosine + x1 * sine], 0)

    load_k.wait()
    for g in range(2):
        k_turned = turned(k_nat[:, g * HEAD : (g + 1) * HEAD].astype(F32).T)
        k_t[g, :, 0:ROWS] = k_turned.astype(BF16)
        k_all[g, 0:ROWS] = k_turned.T.astype(BF16)
        if g == 0:
            next_k(0).start()
    load_v1.wait()
    for g in range(2):
        v_t[g, :, 0:ROWS] = v_all[g, 0:ROWS].astype(F32).T.astype(BF16)

    k_pos = jnp.broadcast_to(q_pos, (8, ROWS)).T[:, 0:1]

    def hidden(step, a, b):
        return jnp.where(codes[0, step, a, b] == 1, 0.0, HIDDEN).astype(F32)

    for a in range(2):
        code = codes[0, 0, a, a]
        early = k_pos[a * HALF : (a + 1) * HALF] <= q_pos[:, a * HALF : (a + 1) * HALF]
        shown = jnp.where(early, jnp.where(code >= 1, 0.0, HIDDEN), jnp.where(code == 1, 0.0, HIDDEN))
        diag[a] = shown.astype(F32)

    load_q.wait()

    def turn_queries(h, carry):
        x = q_nat[:, pl.ds(pl.multiple_of(h * HEAD, HEAD), HEAD)].astype(F32).T
        q_t[h] = turned(x).astype(BF16)
        return carry

    lax.fori_loop(0, HEADS, turn_queries, 0)

    def forward_own(i, carry):
        heads = [i * AT_ONCE + u for u in range(AT_ONCE)]
        g = heads[0] // 4

        raws = [dot(k_all[g, 0:ROWS], q_t[h]) for h in heads]
        rounded = []
        for h, raw in zip(heads, raws):
            columns = []
            for a in range(2):
                cols = slice(a * HALF, (a + 1) * HALF)
                same = raw[cols, cols] + diag[a]
                other = raw[(1 - a) * HALF : (2 - a) * HALF, cols]
                off = hidden(0, a, 1 - a)
                top = jnp.maximum(
                    jnp.max(same, 0, keepdims=True), jnp.max(other, 0, keepdims=True) + off
                )
                shift = top * -POWER
                same = jnp.exp2(same * POWER + shift)
                other = jnp.exp2(other * POWER + (shift + off))
                total = jnp.sum(same, 0, keepdims=True) + jnp.sum(other, 0, keepdims=True)
                stats[h, 0:1, cols] = top
                stats[h, 1:2, cols] = total
                pair = [same, other] if a == 0 else [other, same]
                columns.append(jnp.concatenate(pair, 0).astype(BF16))
            rounded.append(jnp.concatenate(columns, 1))
        for h, e in zip(heads, rounded):
            weights[h, 0:ROWS] = e
            attn_own[h] = dot(v_t[g, :, 0:ROWS], e)
        return carry

    lax.fori_loop(0, HEADS // AT_ONCE, forward_own, 0)

    next_v(0).wait_send()
    next_k(0).wait_send()
    next_v(1).start()
    next_k(1).start()
    load_og.wait()
    load_up.wait()
    load_down.wait()
    back_t[...] = dot_nt(up[...], og[...]).astype(BF16)
    down[...] = down_t[...].astype(F32).T.astype(BF16)
    load_w.wait()

    def project(i, carry):
        at = pl.multiple_of(i * 512, 512)
        x = dot_nt(w[pl.ds(at, 512)], og[...]) + 2.0 * dot(down[pl.ds(at, 512)], back_t[...])
        d_attn_t[pl.ds(i * 4, 4)] = x.astype(BF16).reshape(4, HEAD, ROWS)
        return carry

    lax.fori_loop(0, 2, project, 0)

    def take_previous(g):
        next_v(g).wait_recv()
        next_k(g).wait_recv()
        k_t[g, :, ROWS : 2 * ROWS] = k_all[g, ROWS : 2 * ROWS].astype(F32).T.astype(BF16)
        v_t[g, :, ROWS : 2 * ROWS] = v_all[g, ROWS : 2 * ROWS].astype(F32).T.astype(BF16)

    def forward_previous(i, carry):
        heads = [i * AT_ONCE + u for u in range(AT_ONCE)]
        g = heads[0] // 4

        @pl.when(heads[0] == 0)
        def _():
            take_previous(0)

        @pl.when(heads[0] == 4)
        def _():
            next_v(1).wait_send()
            next_k(1).wait_send()
            take_previous(1)

        raws = [dot(k_all[g, ROWS : 2 * ROWS], q_t[h]) for h in heads]
        rounded, factors = [], []
        for h, raw in zip(heads, raws):
            columns, pairs = [], []
            for a in range(2):
                cols = slice(a * HALF, (a + 1) * HALF)
                first, second = raw[0:HALF, cols], raw[HALF:ROWS, cols]
                off1, off2 = hidden(1, a, 0), hidden(1, a, 1)
                top = jnp.maximum(
                    jnp.max(first, 0, keepdims=True) + off1, jnp.max(second, 0, keepdims=True) + off2
                )
                shift = jnp.minimum(top * -POWER, 1e28)
                first = jnp.exp2(first * POWER + (shift + off1))
                second = jnp.exp2(second * POWER + (shift + off2))
                total = jnp.sum(first, 0, keepdims=True) + jnp.sum(second, 0, keepdims=True)
                top_own = stats[h, 0:1, cols]
                top_all = jnp.maximum(top, top_own)
                own = jnp.exp2((top_own - top_all) * POWER)
                previous = jnp.exp2((top - top_all) * POWER)
                share = 1.0 / (stats[h, 1:2, cols] * own + total * previous)
                own, previous = own * share, previous * share
                stats[h, 2:3, cols] = own
                stats[h, 3:4, cols] = previous
                columns.append(jnp.concatenate([first, second], 0).astype(BF16))
                pairs.append((own, previous))
            rounded.append(jnp.concatenate(columns, 1))
            factors.append([jnp.concatenate(x, 1) for x in zip(*pairs)])
        for h, e, (own, previous) in zip(heads, rounded, factors):
            weights[h, ROWS : 2 * ROWS] = e
            part = dot(v_t[g, :, ROWS : 2 * ROWS], e)
            attn_t[h] = (attn_own[h] * own + part * previous).astype(BF16)
        return carry

    lax.fori_loop(0, HEADS // AT_ONCE, forward_previous, 0)

    mid_part = dot(down_t[...], attn_t[...].reshape(HEADS * HEAD, ROWS))
    mid_own[...] = mid_part.astype(BF16)
    begin(mids())
    for h in range(HEADS):
        part_a[h] = dot_nt(back_t[...], attn_t[h]).astype(BF16)
    begin(rs1_a())

    def backward(t, g):
        rows = slice(t * ROWS, (t + 1) * ROWS)
        heads = range(g * 4, g * 4 + 4)
        d_weights = [dot(v_all[g, rows], d_attn_t[h]) for h in heads]
        d_scores, scaled = [], []
        for h, d_weight in zip(heads, d_weights):
            grad = d_attn_t[h].astype(F32)
            factor = stats[h, 2 + t : 3 + t]
            if t == 1:
                stats[h, 4:5] = jnp.sum(grad * attn_t[h].astype(F32), 0, keepdims=True)
            delta = stats[h, 4:5]
            p = weights[h, rows].astype(F32)
            d_scores.append((p * (d_weight * factor - delta * factor)).astype(BF16))
            scaled.append((grad * factor).astype(BF16))
        dk = [dot_nt(x, q_t[h]) for h, x in zip(heads, d_scores)]
        dv = [dot_nt(weights[h, rows], x) for h, x in zip(heads, scaled)]
        dk, dv = sum(dk[1:], dk[0]) * SCALE, sum(dv[1:], dv[0])
        if t == 1:
            back_send[g, 0] = dk.astype(BF16)
            back_send[g, 1] = dv.astype(BF16)
            back_copy(g).start()
        else:
            dk_acc[g] = dk
            dv_acc[g] = dv
        for h, x in zip(heads, d_scores):
            dq = dot(k_t[g, :, rows], x)
            if t == 1:
                attn_own[h] = dq
            else:
                dq = (dq + attn_own[h]) * SCALE
                x1, x2 = dq[:64], dq[64:]
                dq = jnp.concatenate([x1 * cosine + x2 * sine, x2 * cosine - x1 * sine], 0)
                dq_out[:, h * HEAD : (h + 1) * HEAD] = dq.T.astype(BF16)

    def finish_keys(g):
        back_copy(g).wait()
        x = (dk_acc[g] + back_recv[g, 0].astype(F32)).T
        x1, x2 = x[:64], x[64:]
        x = jnp.concatenate([x1 * cosine + x2 * sine, x2 * cosine - x1 * sine], 0)
        dk_out[:, g * HEAD : (g + 1) * HEAD] = x.T.astype(BF16)
        dv = dv_acc[g] + back_recv[g, 1].astype(F32)
        dv_out[:, g * HEAD : (g + 1) * HEAD] = dv.astype(BF16)

    stores = [
        pltpu.make_async_copy(src, dst, store_sem.at[i])
        for i, (src, dst) in enumerate([
            (dq_out.at[:, 0:512], dq_hbm.at[:, 0:512]),
            (dq_out.at[:, 512:1024], dq_hbm.at[:, 512:1024]),
            (dk_out, dk_hbm), (dv_out, dv_hbm), (a_out, a_hbm),
        ])
    ]

    backward(1, 0)
    finish(mids())
    mid = mid_part
    for o in range(1, 4):
        mid = mid + mid_all[o].astype(F32)
    b_part = dot(mid.astype(BF16), og[:, pl.ds(pl.multiple_of(r * 1024, 1024), 1024)])
    for c in range(8):
        part_b[c] = b_part[:, c * HEAD : (c + 1) * HEAD].astype(BF16)
    begin(rs1_b())

    backward(1, 1)
    finish(rs1_a())
    finish(rs1_b())
    total_a, total_b = part_a[z].astype(F32), part_b[z].astype(F32)
    for o in range(1, 8):
        total_a = total_a + rs1a[o].astype(F32)
        total_b = total_b + rs1b[o].astype(F32)
    all_j[j, 0:32] = total_a.astype(BF16)
    all_j[j, 32:64] = total_b.astype(BF16)
    begin(all_j_copies())

    backward(0, 0)
    stores[0].start()
    finish(all_j_copies())
    total = all_j[0].astype(F32)
    for o in range(1, 8):
        total = total + all_j[o].astype(F32)
    full[z] = (2.0 * total).astype(BF16)
    begin([ag2(o) for o in range(1, 8)])
    begin(ag3(0))

    backward(0, 1)
    stores[1].start()
    for o in range(1, 8):
        ag2(o).wait()
        begin(ag3(o))
    b_all[r] = full[:, 32:64, :]
    for c in range(8):
        a_out[:, c * HEAD : (c + 1) * HEAD] = full[c, 0:32].astype(F32)
    stores[4].start()
    finish_keys(0)
    finish_keys(1)
    stores[2].start()
    stores[3].start()
    for k in range(8):
        finish(ag3(k))
    b_out[...] = b_all[...]
    finish(stores)


def write_kernel(
    dq, dk, dv, a, b, dq_out, dk_out, dv_out, a_out, b_out,
    dq_in, dk_in, dv_in, a_in, b_in, b_wide, in_sem, out_sem,
):
    quarter = ROWS // 4
    steps = [(dk, dk_in, dk_out), (dv, dv_in, dv_out), (a, a_in, a_out)]
    for i in range(4):
        rows = slice(i * quarter, (i + 1) * quarter)
        steps.append((dq.at[rows], dq_in.at[rows], dq_out.at[rows]))
    loads = [pltpu.make_async_copy(x, y, in_sem.at[i]) for i, (x, y, _) in enumerate(steps)]
    stores = [pltpu.make_async_copy(y, o, out_sem.at[i]) for i, (_, y, o) in enumerate(steps)]
    load_b = pltpu.make_async_copy(b, b_in, in_sem.at[7])
    store_b = pltpu.make_async_copy(b_wide, b_out, out_sem.at[7])
    load_b.start()
    for copy in loads:
        copy.start()
    load_b.wait()
    for p in range(4):
        for c in range(8):
            at = p * 1024 + c * HEAD
            b_wide[:, at : at + HEAD] = b_in[p, c].astype(F32)
    store_b.start()
    for load, store in zip(loads, stores):
        load.wait()
        store.start()
    for copy in stores:
        copy.wait()
    store_b.wait()


def shards(
    queries,
    keys,
    values,
    output_gradient,
    output_weight,
    adapter_down,
    adapter_up,
    positions,
    block_pair_mask,
):
    vmem = pl.BlockSpec(memory_space=pltpu.VMEM)
    smem = pl.BlockSpec(memory_space=pltpu.SMEM)
    hbm = pl.BlockSpec(memory_space=pl.ANY)
    out = jax.ShapeDtypeStruct
    dq, dk, dv, a, b = pl.pallas_call(
        layer_kernel,
        out_shape=(
            out((ROWS, HEADS * HEAD), BF16),
            out((ROWS, 2 * HEAD), BF16),
            out((ROWS, 2 * HEAD), BF16),
            out((32, HEADS * HEAD), F32),
            out((4, 8, 32, HEAD), BF16),
        ),
        in_specs=[hbm] * 7 + [vmem, vmem, smem],
        out_specs=(hbm,) * 4 + (vmem,),
        scratch_shapes=[
            pltpu.VMEM((ROWS, 2 * HEAD), BF16),
            pltpu.VMEM((32, WIDTH), BF16),
            pltpu.VMEM((32, HEADS * HEAD), BF16),
            pltpu.VMEM((2, 64, ROWS), F32),
            pltpu.VMEM((ROWS, HEADS * HEAD), BF16),
            pltpu.VMEM((ROWS, 2 * HEAD), BF16),
            pltpu.VMEM((ROWS, 2 * HEAD), BF16),
            pltpu.VMEM((32, HEADS * HEAD), F32),
            pltpu.VMEM((ROWS, HEADS * HEAD), BF16),
            pltpu.VMEM((ROWS, WIDTH), BF16),
            pltpu.VMEM((HEADS * HEAD, WIDTH), BF16),
            pltpu.VMEM((2, 2 * ROWS, HEAD), BF16),
            pltpu.VMEM((2, 2 * ROWS, HEAD), BF16),
            pltpu.VMEM((2, HEAD, 2 * ROWS), BF16),
            pltpu.VMEM((2, HEAD, 2 * ROWS), BF16),
            pltpu.VMEM((HEADS, HEAD, ROWS), BF16),
            pltpu.VMEM((2, HALF, HALF), F32),
            pltpu.VMEM((HEADS, 2 * ROWS, ROWS), BF16),
            pltpu.VMEM((HEADS, 8, ROWS), F32),
            pltpu.VMEM((HEADS, HEAD, ROWS), F32),
            pltpu.VMEM((HEADS, HEAD, ROWS), BF16),
            pltpu.VMEM((HEADS, HEAD, ROWS), BF16),
            pltpu.VMEM((32, ROWS), BF16),
            pltpu.VMEM((HEADS * HEAD, 32), BF16),
            pltpu.VMEM((2, ROWS, HEAD), F32),
            pltpu.VMEM((2, ROWS, HEAD), F32),
            pltpu.VMEM((32, ROWS), BF16),
            pltpu.VMEM((4, 32, ROWS), BF16),
            pltpu.VMEM((2, 2, ROWS, HEAD), BF16),
            pltpu.VMEM((2, 2, ROWS, HEAD), BF16),
            pltpu.VMEM((8, 32, HEAD), BF16),
            pltpu.VMEM((8, 32, HEAD), BF16),
            pltpu.VMEM((8, 32, HEAD), BF16),
            pltpu.VMEM((8, 32, HEAD), BF16),
            pltpu.VMEM((8, 64, HEAD), BF16),
            pltpu.VMEM((8, 64, HEAD), BF16),
            pltpu.VMEM((4, 8, 32, HEAD), BF16),
            pltpu.SemaphoreType.DMA((8,)),
            pltpu.SemaphoreType.DMA((5,)),
            pltpu.SemaphoreType.DMA((COPIES,)),
            pltpu.SemaphoreType.DMA((COPIES,)),
        ],
        compiler_params=pltpu.CompilerParams(
            collective_id=0, has_side_effects=True, vmem_limit_bytes=56 * 1024 * 1024
        ),
    )(
        queries,
        keys,
        values,
        output_gradient,
        output_weight,
        adapter_down.T,
        adapter_up,
        jnp.broadcast_to(FREQUENCY[:, None], (64, HEAD)),
        positions[None, :],
        block_pair_mask,
    )
    dq, dk, dv, a, b = pl.pallas_call(
        write_kernel,
        out_shape=(
            out((ROWS, HEADS * HEAD), BF16),
            out((ROWS, 2 * HEAD), BF16),
            out((ROWS, 2 * HEAD), BF16),
            out((32, HEADS * HEAD), F32),
            out((32, WIDTH), F32),
        ),
        in_specs=[hbm] * 5,
        out_specs=(hbm,) * 5,
        scratch_shapes=[
            pltpu.VMEM((ROWS, HEADS * HEAD), BF16),
            pltpu.VMEM((ROWS, 2 * HEAD), BF16),
            pltpu.VMEM((ROWS, 2 * HEAD), BF16),
            pltpu.VMEM((32, HEADS * HEAD), F32),
            pltpu.VMEM((4, 8, 32, HEAD), BF16),
            pltpu.VMEM((32, WIDTH), F32),
            pltpu.SemaphoreType.DMA((8,)),
            pltpu.SemaphoreType.DMA((8,)),
        ],
    )(dq, dk, dv, a, b)
    return dq, dk, dv, a.T, b


def solution(mesh):
    placed = (
        P("seq", "rep"),
        P("seq", "rep"),
        P("seq", "rep"),
        P("seq", None),
        P("rep", None),
        P("rep", None),
        P(),
        P("seq"),
        P("seq", None, None, None),
    )
    return jax.shard_map(
        shards,
        mesh=mesh,
        in_specs=placed,
        out_specs=(P("seq", "rep"), P("seq", "rep"), P("seq", "rep"), P("rep", None), P()),
        check_vma=False,
    )
```

time: 68.9 us -> 62.5 us (0.907)
  Pallas kernels: 66.2 us -> 59.7 us
  other arithmetic: 1.93 us -> 0 us
  local copies, waits for them, and re-layouts: 0 us -> 1.35 us
    pallas_call x1, Pallas kernels: 63.7 us -> 57.2 us  [shards(): pl.pallas_call(layer_kernel, out_shape=(out((ROWS, HEADS * HEAD), BF16),...]
    broadcast_in_dim x0 -> x1, local copies, waits for them, and re-layouts: none -> 1.35 us  [shards(): jnp.broadcast_to(FREQUENCY[:, None], (64, HEAD))]
    sin x1 -> x0, other arithmetic: 1.24 us -> none  [shards(): jnp.sin(phase)]
where the time goes in v3:
time: 62.5 us; the launch traced here: 61.8 us
  Pallas kernels  59.7 us (96%)
  local copies, waits for them, and re-layouts  1.35 us (2%)
  between operations  0.8 us (1%)
    pallas_call x1, Pallas kernels, shards(): pl.pallas_call(layer_kernel, out_shape=(out((ROWS, HEADS * HEAD), BF16),...  57.2 us
    pallas_call x1, Pallas kernels, shards(): pl.pallas_call(write_kernel, out_shape=(out((ROWS, HEADS * HEAD), BF16),...  2.48 us
    broadcast_in_dim x1, local copies, waits for them, and re-layouts, shards(): jnp.broadcast_to(FREQUENCY[:, None], (64, HEAD))  1.35 us

profile of v3, /device:TPU:24, one launch (start us, length us, event | category | flops | bytes accessed | tf_op | source)
XLA Modules:
  0.0 61.8 jit_solution(6208710385722329100)
XLA Ops:
  0.6 1.3 %broadcast_in_dim.11.freq = f32[64,128]{1,0:T(8,128)} broadcast(f32[64]{0:T(128)} %constant.4), dimensions={0} | broadcast | bytes 33024 | tf_op jit(solution)/shard_map/broadcast_in_dim | solution.py:484
  2.0 57.2 %shard_map.137 = (bf16[512,1024]{1,0:T(8,128)(2,1)}, bf16[512,256]{1,0:T(8,128)(2,1)}, bf16[512,256]{1,0:T(8,128)(2,1)}, f32[32,1024]{1,0:T(8,128)}, bf16[4,8,32,128]{3,2,1,0:T(8,128)(2,1)}) custom-call(bf16[512,1024]{1,0:T(8,128)(2,1)} %q_hbm.1, bf16[512,256]{1,0:T(8,128)(2,1)} %k_hbm.1, bf16[512,256]{1,0:T(8,128)(2,1)} %v_hbm.1, bf16[512,4096]{1,0:T(8,128)(2,1)} %og_hbm.1, ...), custom_call_target="tpu_custom_call" | custom-call | tf_op jit(solution)/shard_map/pallas_call | solution.py:419
  59.2 2.5 %shard_map.138 = (bf16[512,1024]{1,0:T(8,128)(2,1)}, bf16[512,256]{1,0:T(8,128)(2,1)}, bf16[512,256]{1,0:T(8,128)(2,1)}, f32[32,1024]{1,0:T(8,128)}, f32[32,4096]{1,0:T(8,128)}) custom-call(bf16[512,1024]{1,0:T(8,128)(2,1)} %get-tuple-element.15.dq, bf16[512,256]{1,0:T(8,128)(2,1)} %get-tuple-element.16.dk, bf16[512,256]{1,0:T(8,128)(2,1)} %get-tuple-element.17.dv, ...), custom_call_target="tpu_custom_call" | custom-call | tf_op jit(solution)/shard_map/pallas_call | solution.py:488

commit v4 on v3

--- a/solution.py
+++ b/solution.py
@@ -190,7 +190,6 @@
 
     next_v(0).wait_send()
     next_k(0).wait_send()
-    next_v(1).start()
     next_k(1).start()
     load_og.wait()
     load_up.wait()
@@ -205,32 +204,15 @@
         d_attn_t[pl.ds(i * 4, 4)] = x.astype(BF16).reshape(4, HEAD, ROWS)
         return carry
 
-    lax.fori_loop(0, 2, project, 0)
-
-    def take_previous(g):
-        next_v(g).wait_recv()
-        next_k(g).wait_recv()
-        k_t[g, :, ROWS : 2 * ROWS] = k_all[g, ROWS : 2 * ROWS].astype(F32).T.astype(BF16)
-        v_t[g, :, ROWS : 2 * ROWS] = v_all[g, ROWS : 2 * ROWS].astype(F32).T.astype(BF16)
-
-    def forward_previous(i, carry):
-        heads = [i * AT_ONCE + u for u in range(AT_ONCE)]
-        g = heads[0] // 4
-
-        @pl.when(heads[0] == 0)
-        def _():
-            take_previous(0)
-
-        @pl.when(heads[0] == 4)
-        def _():
-            next_v(1).wait_send()
-            next_k(1).wait_send()
-            take_previous(1)
-
+    project(0, 0)
+    next_k(1).wait_send()
+    next_v(1).start()
+
+    def previous_scores(g):
+        heads = range(g * 4, g * 4 + 4)
         raws = [dot(k_all[g, ROWS : 2 * ROWS], q_t[h]) for h in heads]
-        rounded, factors = [], []
         for h, raw in zip(heads, raws):
-            columns, pairs = [], []
+            columns = []
             for a in range(2):
                 cols = slice(a * HALF, (a + 1) * HALF)
                 first, second = raw[0:HALF, cols], raw[HALF:ROWS, cols]
@@ -251,16 +233,22 @@
                 stats[h, 2:3, cols] = own
                 stats[h, 3:4, cols] = previous
                 columns.append(jnp.concatenate([first, second], 0).astype(BF16))
-                pairs.append((own, previous))
-            rounded.append(jnp.concatenate(columns, 1))
-            factors.append([jnp.concatenate(x, 1) for x in zip(*pairs)])
-        for h, e, (own, previous) in zip(heads, rounded, factors):
-            weights[h, ROWS : 2 * ROWS] = e
-            part = dot(v_t[g, :, ROWS : 2 * ROWS], e)
-            attn_t[h] = (attn_own[h] * own + part * previous).astype(BF16)
-        return carry
-
-    lax.fori_loop(0, HEADS // AT_ONCE, forward_previous, 0)
+            weights[h, ROWS : 2 * ROWS] = jnp.concatenate(columns, 1)
+
+    def previous_values(g):
+        v_t[g, :, ROWS : 2 * ROWS] = v_all[g, ROWS : 2 * ROWS].astype(F32).T.astype(BF16)
+        for h in range(g * 4, g * 4 + 4):
+            part = dot(v_t[g, :, ROWS : 2 * ROWS], weights[h, ROWS : 2 * ROWS])
+            attn_t[h] = (attn_own[h] * stats[h, 2:3] + part * stats[h, 3:4]).astype(BF16)
+
+    next_k(0).wait_recv()
+    next_v(0).wait_recv()
+    previous_scores(0)
+    previous_values(0)
+    next_k(1).wait_recv()
+    previous_scores(1)
+    next_v(1).wait()
+    previous_values(1)
 
     mid_part = dot(down_t[...], attn_t[...].reshape(HEADS * HEAD, ROWS))
     mid_own[...] = mid_part.astype(BF16)
@@ -289,7 +277,6 @@
         if t == 1:
             back_send[g, 0] = dk.astype(BF16)
             back_send[g, 1] = dv.astype(BF16)
-            back_copy(g).start()
         else:
             dk_acc[g] = dk
             dv_acc[g] = dv
@@ -321,7 +308,10 @@
         ])
     ]
 
+    for g in range(2):
+        k_t[g, :, ROWS : 2 * ROWS] = k_all[g, ROWS : 2 * ROWS].astype(F32).T.astype(BF16)
     backward(1, 0)
+    back_copy(0).start()
     finish(mids())
     mid = mid_part
     for o in range(1, 4):
@@ -331,7 +321,7 @@
         part_b[c] = b_part[:, c * HEAD : (c + 1) * HEAD].astype(BF16)
     begin(rs1_b())
 
-    backward(1, 1)
+    project(1, 0)
     finish(rs1_a())
     finish(rs1_b())
     total_a, total_b = part_a[z].astype(F32), part_b[z].astype(F32)
@@ -342,8 +332,7 @@
     all_j[j, 32:64] = total_b.astype(BF16)
     begin(all_j_copies())
 
-    backward(0, 0)
-    stores[0].start()
+    backward(1, 1)
     finish(all_j_copies())
     total = all_j[0].astype(F32)
     for o in range(1, 8):
@@ -351,9 +340,10 @@
     full[z] = (2.0 * total).astype(BF16)
     begin([ag2(o) for o in range(1, 8)])
     begin(ag3(0))
-
-    backward(0, 1)
-    stores[1].start()
+    back_copy(1).start()
+
+    backward(0, 0)
+    stores[0].start()
     for o in range(1, 8):
         ag2(o).wait()
         begin(ag3(o))
@@ -361,6 +351,8 @@
     for c in range(8):
         a_out[:, c * HEAD : (c + 1) * HEAD] = full[c, 0:32].astype(F32)
     stores[4].start()
+    backward(0, 1)
+    stores[1].start()
     finish_keys(0)
     finish_keys(1)
     stores[2].start()

time: 62.5 us -> 58.8 us (0.941)
  Pallas kernels: 59.7 us -> 55.9 us
    pallas_call x1, Pallas kernels: 57.2 us -> 53.4 us  [shards(): pl.pallas_call(layer_kernel, out_shape=(out((ROWS, HEADS * HEAD), BF16),...]
where the time goes in v4:
time: 58.8 us; the launch traced here: 58 us
  Pallas kernels  55.9 us (95%)
  local copies, waits for them, and re-layouts  1.35 us (2%)
  between operations  0.82 us (1%)
    pallas_call x1, Pallas kernels, shards(): pl.pallas_call(layer_kernel, out_shape=(out((ROWS, HEADS * HEAD), BF16),...  53.4 us
    pallas_call x1, Pallas kernels, shards(): pl.pallas_call(write_kernel, out_shape=(out((ROWS, HEADS * HEAD), BF16),...  2.48 us
    broadcast_in_dim x1, local copies, waits for them, and re-layouts, shards(): jnp.broadcast_to(FREQUENCY[:, None], (64, HEAD))  1.35 us

profile of v4, /device:TPU:24, one launch (start us, length us, event | category | flops | bytes accessed | tf_op | source)
XLA Modules:
  0.0 58.0 jit_solution(2569092153770003436)
XLA Ops:
  0.6 1.3 %broadcast_in_dim.11.freq = f32[64,128]{1,0:T(8,128)} broadcast(f32[64]{0:T(128)} %constant.4), dimensions={0} | broadcast | bytes 33024 | tf_op jit(solution)/shard_map/broadcast_in_dim | solution.py:476
  2.0 53.4 %shard_map.137 = (bf16[512,1024]{1,0:T(8,128)(2,1)}, bf16[512,256]{1,0:T(8,128)(2,1)}, bf16[512,256]{1,0:T(8,128)(2,1)}, f32[32,1024]{1,0:T(8,128)}, bf16[4,8,32,128]{3,2,1,0:T(8,128)(2,1)}) custom-call(bf16[512,1024]{1,0:T(8,128)(2,1)} %q_hbm.1, bf16[512,256]{1,0:T(8,128)(2,1)} %k_hbm.1, bf16[512,256]{1,0:T(8,128)(2,1)} %v_hbm.1, bf16[512,4096]{1,0:T(8,128)(2,1)} %og_hbm.1, ...), custom_call_target="tpu_custom_call" | custom-call | tf_op jit(solution)/shard_map/pallas_call | solution.py:411
  55.4 2.5 %shard_map.138 = (bf16[512,1024]{1,0:T(8,128)(2,1)}, bf16[512,256]{1,0:T(8,128)(2,1)}, bf16[512,256]{1,0:T(8,128)(2,1)}, f32[32,1024]{1,0:T(8,128)}, f32[32,4096]{1,0:T(8,128)}) custom-call(bf16[512,1024]{1,0:T(8,128)(2,1)} %get-tuple-element.15.dq, bf16[512,256]{1,0:T(8,128)(2,1)} %get-tuple-element.16.dk, bf16[512,256]{1,0:T(8,128)(2,1)} %get-tuple-element.17.dv, ...), custom_call_target="tpu_custom_call" | custom-call | tf_op jit(solution)/shard_map/pallas_call | solution.py:480

commit v5 on v4

--- a/solution.py
+++ b/solution.py
@@ -18,7 +18,7 @@
 POWER = SCALE * 1.4426950408889634
 HIDDEN = -1e30
 AT_ONCE = 4
-FREQUENCY = (1000000.0 ** (-np.arange(64) * 2.0 / 128)).astype(np.float32)
+FREQUENCY = [float(np.float32(1000000.0 ** (-i * 2.0 / 128))) for i in range(64)]
 
 K_NEXT, V_NEXT, MID, RS1A, RS1B, ALLJ, AG2, BACK, AG3, COPIES = 0, 2, 4, 8, 16, 24, 32, 40, 42, 74
 
@@ -36,9 +36,9 @@
 
 
 def layer_kernel(
-    q_hbm, k_hbm, v_hbm, og_hbm, w_hbm, down_hbm, up_hbm, freq, pos_row, codes,
-    dq_hbm, dk_hbm, dv_hbm, a_hbm, b_out,
-    k_nat, up, down_t, angle, dq_out, dk_out, dv_out, a_out,
+    q_hbm, k_hbm, v_hbm, og_hbm, w_hbm, down_hbm, up_hbm, pos_hbm, codes_hbm,
+    dq_hbm, dk_hbm, dv_hbm, a_hbm, b_hbm,
+    pos_row, codes, k_nat, up, down_t, angle, dq_out, dk_out, dv_out, a_out,
     q_nat, og, w, k_all, v_all, k_t, v_t, q_t, diag, weights, stats, attn_own, attn_t, d_attn_t, back_t, down,
     dk_acc, dv_acc, mid_own, mid_all, back_send, back_recv,
     part_a, part_b, rs1a, rs1b, all_j, full, b_all,
@@ -106,15 +106,20 @@
     for at, (src, dst) in enumerate([
         (v_hbm.at[:, 0:HEAD], v_all.at[0, 0:ROWS]),
         (v_hbm.at[:, HEAD : 2 * HEAD], v_all.at[1, 0:ROWS]),
-        (k_hbm, k_nat), (q_hbm, q_nat), (og_hbm, og), (up_hbm, up), (down_hbm, down_t), (w_hbm, w),
+        (pos_hbm, pos_row), (codes_hbm, codes), (k_hbm, k_nat), (q_hbm, q_nat), (og_hbm, og), (up_hbm, up), (down_hbm, down_t), (w_hbm, w),
     ]):
         loads.append(pltpu.make_async_copy(src, dst, load_sem.at[at]))
         loads[at].start()
-    load_v0, load_v1, load_k, load_q, load_og, load_up, load_down, load_w = loads
-
+    load_v0, load_v1, load_pos, load_codes, load_k, load_q, load_og, load_up, load_down, load_w = loads
+
+    row = lax.broadcasted_iota(jnp.int32, (64, HEAD), 0)
+    freq = jnp.zeros((64, HEAD), F32)
+    for i in range(64):
+        freq = jnp.where(row == i, FREQUENCY[i], freq)
     load_v0.wait()
     pl.semaphore_wait(barrier, len(peers))
     next_v(0).start()
+    load_pos.wait()
     q_pos = pos_row[...].astype(F32)
     phase = freq[:, 0:1] * q_pos
     angle[0] = jnp.cos(phase)
@@ -130,12 +135,12 @@
         k_turned = turned(k_nat[:, g * HEAD : (g + 1) * HEAD].astype(F32).T)
         k_t[g, :, 0:ROWS] = k_turned.astype(BF16)
         k_all[g, 0:ROWS] = k_turned.T.astype(BF16)
-        if g == 0:
-            next_k(0).start()
+        next_k(g).start()
     load_v1.wait()
     for g in range(2):
         v_t[g, :, 0:ROWS] = v_all[g, 0:ROWS].astype(F32).T.astype(BF16)
 
+    load_codes.wait()
     k_pos = jnp.broadcast_to(q_pos, (8, ROWS)).T[:, 0:1]
 
     def hidden(step, a, b):
@@ -188,9 +193,7 @@
 
     lax.fori_loop(0, HEADS // AT_ONCE, forward_own, 0)
 
-    next_v(0).wait_send()
-    next_k(0).wait_send()
-    next_k(1).start()
+    next_v(1).start()
     load_og.wait()
     load_up.wait()
     load_down.wait()
@@ -205,8 +208,6 @@
         return carry
 
     project(0, 0)
-    next_k(1).wait_send()
-    next_v(1).start()
 
     def previous_scores(g):
         heads = range(g * 4, g * 4 + 4)
@@ -241,11 +242,11 @@
             part = dot(v_t[g, :, ROWS : 2 * ROWS], weights[h, ROWS : 2 * ROWS])
             attn_t[h] = (attn_own[h] * stats[h, 2:3] + part * stats[h, 3:4]).astype(BF16)
 
-    next_k(0).wait_recv()
-    next_v(0).wait_recv()
+    next_k(0).wait()
+    next_v(0).wait()
     previous_scores(0)
     previous_values(0)
-    next_k(1).wait_recv()
+    next_k(1).wait()
     previous_scores(1)
     next_v(1).wait()
     previous_values(1)
@@ -359,8 +360,10 @@
     stores[3].start()
     for k in range(8):
         finish(ag3(k))
-    b_out[...] = b_all[...]
+    store_b = pltpu.make_async_copy(b_all, b_hbm, store_sem.at[5])
+    store_b.start()
     finish(stores)
+    store_b.wait()
 
 
 def write_kernel(
@@ -404,8 +407,7 @@
     positions,
     block_pair_mask,
 ):
-    vmem = pl.BlockSpec(memory_space=pltpu.VMEM)
-    smem = pl.BlockSpec(memory_space=pltpu.SMEM)
+    anywhere = pl.BlockSpec(memory_space=pl.ANY)
     hbm = pl.BlockSpec(memory_space=pl.ANY)
     out = jax.ShapeDtypeStruct
     dq, dk, dv, a, b = pl.pallas_call(
@@ -417,9 +419,11 @@
             out((32, HEADS * HEAD), F32),
             out((4, 8, 32, HEAD), BF16),
         ),
-        in_specs=[hbm] * 7 + [vmem, vmem, smem],
-        out_specs=(hbm,) * 4 + (vmem,),
+        in_specs=[hbm] * 9,
+        out_specs=(anywhere,) * 5,
         scratch_shapes=[
+            pltpu.VMEM((1, ROWS), jnp.int32),
+            pltpu.SMEM((1, 2, 2, 2), jnp.int32),
             pltpu.VMEM((ROWS, 2 * HEAD), BF16),
             pltpu.VMEM((32, WIDTH), BF16),
             pltpu.VMEM((32, HEADS * HEAD), BF16),
@@ -457,8 +461,8 @@
             pltpu.VMEM((8, 64, HEAD), BF16),
             pltpu.VMEM((8, 64, HEAD), BF16),
             pltpu.VMEM((4, 8, 32, HEAD), BF16),
-            pltpu.SemaphoreType.DMA((8,)),
-            pltpu.SemaphoreType.DMA((5,)),
+            pltpu.SemaphoreType.DMA((10,)),
+            pltpu.SemaphoreType.DMA((6,)),
             pltpu.SemaphoreType.DMA((COPIES,)),
             pltpu.SemaphoreType.DMA((COPIES,)),
         ],
@@ -473,7 +477,6 @@
         output_weight,
         adapter_down.T,
         adapter_up,
-        jnp.broadcast_to(FREQUENCY[:, None], (64, HEAD)),
         positions[None, :],
         block_pair_mask,
     )
@@ -486,8 +489,8 @@
             out((32, HEADS * HEAD), F32),
             out((32, WIDTH), F32),
         ),
-        in_specs=[hbm] * 5,
-        out_specs=(hbm,) * 5,
+        in_specs=[anywhere] * 5,
+        out_specs=(anywhere,) * 5,
         scratch_shapes=[
             pltpu.VMEM((ROWS, HEADS * HEAD), BF16),
             pltpu.VMEM((ROWS, 2 * HEAD), BF16),

time: 58.8 us -> 55.2 us (0.939)
  Pallas kernels: 55.9 us -> 53.4 us
  local copies, waits for them, and re-layouts: 1.35 us -> 0 us
    pallas_call x1, Pallas kernels: 53.4 us -> 50.9 us  [shards(): pl.pallas_call(layer_kernel, out_shape=(out((ROWS, HEADS * HEAD), BF16),...]
    broadcast_in_dim x1 -> x0, local copies, waits for them, and re-layouts: 1.35 us -> none  [shards(): jnp.broadcast_to(FREQUENCY[:, None], (64, HEAD))]
where the time goes in v5:
time: 55.2 us; the launch traced here: 54.2 us
  Pallas kernels  53.4 us (97%)
  between operations  0.82 us (1%)
    pallas_call x1, Pallas kernels, shards(): pl.pallas_call(layer_kernel, out_shape=(out((ROWS, HEADS * HEAD), BF16),...  50.9 us
    pallas_call x1, Pallas kernels, shards(): pl.pallas_call(write_kernel, out_shape=(out((ROWS, HEADS * HEAD), BF16),...  2.48 us

profile of v5, /device:TPU:24, one launch (start us, length us, event | category | flops | bytes accessed | tf_op | source)
XLA Modules:
  0.0 54.2 jit_solution(13551822754299950142)
XLA Ops:
  0.6 50.9 %shard_map.128 = (bf16[512,1024]{1,0:T(8,128)(2,1)}, bf16[512,256]{1,0:T(8,128)(2,1)}, bf16[512,256]{1,0:T(8,128)(2,1)}, f32[32,1024]{1,0:T(8,128)}, bf16[4,8,32,128]{3,2,1,0:T(8,128)(2,1)}) custom-call(bf16[512,1024]{1,0:T(8,128)(2,1)} %q_hbm.1, bf16[512,256]{1,0:T(8,128)(2,1)} %k_hbm.1, bf16[512,256]{1,0:T(8,128)(2,1)} %v_hbm.1, bf16[512,4096]{1,0:T(8,128)(2,1)} %og_hbm.1, ...), custom_call_target="tpu_custom_call" | custom-call | tf_op jit(solution)/shard_map/pallas_call | solution.py:413
  51.6 2.5 %shard_map.129 = (bf16[512,1024]{1,0:T(8,128)(2,1)}, bf16[512,256]{1,0:T(8,128)(2,1)}, bf16[512,256]{1,0:T(8,128)(2,1)}, f32[32,1024]{1,0:T(8,128)}, f32[32,4096]{1,0:T(8,128)}) custom-call(bf16[512,1024]{1,0:T(8,128)(2,1)} %get-tuple-element.15.dq, bf16[512,256]{1,0:T(8,128)(2,1)} %get-tuple-element.16.dk, bf16[512,256]{1,0:T(8,128)(2,1)} %get-tuple-element.17.dv, ...), custom_call_target="tpu_custom_call" | custom-call | tf_op jit(solution)/shard_map/pallas_call | solution.py:483

commit v6 on v5

--- a/solution.py
+++ b/solution.py
@@ -137,6 +137,7 @@
         k_all[g, 0:ROWS] = k_turned.T.astype(BF16)
         next_k(g).start()
     load_v1.wait()
+    next_v(1).start()
     for g in range(2):
         v_t[g, :, 0:ROWS] = v_all[g, 0:ROWS].astype(F32).T.astype(BF16)
 
@@ -193,7 +194,6 @@
 
     lax.fori_loop(0, HEADS // AT_ONCE, forward_own, 0)
 
-    next_v(1).start()
     load_og.wait()
     load_up.wait()
     load_down.wait()

time: 55.2 us -> 55.1 us (level)
  no operation moved by 1% of the time
where the time goes in v6:
time: 55.1 us; the launch traced here: 54.2 us
  Pallas kernels  53.4 us (97%)
  between operations  0.82 us (1%)
    pallas_call x1, Pallas kernels, shards(): pl.pallas_call(layer_kernel, out_shape=(out((ROWS, HEADS * HEAD), BF16),...  50.9 us
    pallas_call x1, Pallas kernels, shards(): pl.pallas_call(write_kernel, out_shape=(out((ROWS, HEADS * HEAD), BF16),...  2.48 us

profile of v6, /device:TPU:24, one launch (start us, length us, event | category | flops | bytes accessed | tf_op | source)
XLA Modules:
  0.0 54.2 jit_solution(3435459759415044492)
XLA Ops:
  0.6 50.9 %shard_map.128 = (bf16[512,1024]{1,0:T(8,128)(2,1)}, bf16[512,256]{1,0:T(8,128)(2,1)}, bf16[512,256]{1,0:T(8,128)(2,1)}, f32[32,1024]{1,0:T(8,128)}, bf16[4,8,32,128]{3,2,1,0:T(8,128)(2,1)}) custom-call(bf16[512,1024]{1,0:T(8,128)(2,1)} %q_hbm.1, bf16[512,256]{1,0:T(8,128)(2,1)} %k_hbm.1, bf16[512,256]{1,0:T(8,128)(2,1)} %v_hbm.1, bf16[512,4096]{1,0:T(8,128)(2,1)} %og_hbm.1, ...), custom_call_target="tpu_custom_call" | custom-call | tf_op jit(solution)/shard_map/pallas_call | solution.py:413
  51.5 2.5 %shard_map.129 = (bf16[512,1024]{1,0:T(8,128)(2,1)}, bf16[512,256]{1,0:T(8,128)(2,1)}, bf16[512,256]{1,0:T(8,128)(2,1)}, f32[32,1024]{1,0:T(8,128)}, f32[32,4096]{1,0:T(8,128)}) custom-call(bf16[512,1024]{1,0:T(8,128)(2,1)} %get-tuple-element.15.dq, bf16[512,256]{1,0:T(8,128)(2,1)} %get-tuple-element.16.dk, bf16[512,256]{1,0:T(8,128)(2,1)} %get-tuple-element.17.dv, ...), custom_call_target="tpu_custom_call" | custom-call | tf_op jit(solution)/shard_map/pallas_call | solution.py:483
